TPU v7x, 128 devices: a whole 4x4x4 slice. The times are simulated.
128 devices in a mesh: rcv: 8 (over z, core), shot: 16 (over x, y).
Axes of the slice: x: 4, y: 4, z: 4, core: 2. Of those that a mesh axis runs over, the one named last changes fastest.
Arguments:
- data: bfloat16 [4, 4096, 4096], P(None, 'rcv', 'shot'), may hold values from -6 to 6
- traces: float32 [65536, 2048], P(('rcv', 'shot')), may hold values from -6 to 6
- weight: float32 [65536], P(('rcv', 'shot')), may hold values from 0.5 to 2
- dest: int32 [65536, 1], P(('rcv', 'shot')), may hold values from 0 to 127; in each aligned block of 512 rows (0 to 511, 512 to 1023, ...) at most 8 rows name the same one
- bins: int32 [65536], P(('rcv', 'shot')), may hold values from 0 to 131071
Outputs:
- binned: bfloat16 [4, 4096, 4096], P(None, 'rcv', 'shot')
- multiples: float32 [4, 4096, 4096], P(None, 'rcv', 'shot')
Inputs may be any that keep to these rules, and one draw needn't show every extreme that they name: `dest`: among the 512 traces of one device no owner is named more than 8 times; some owner is named exactly 8 times.
All inputs are finite; a program needn't handle non-finite values.
Results may differ from a plain program's by a relative error of at most 0.0014.
Values may be sent and summed in bfloat16 or wider, within the bound.
A program may use at most 320 MiB of HBM per device.

v0:
```python
import math

import jax
import jax.numpy as jnp
from jax import lax
from jax.sharding import PartitionSpec as P

STEPS = 4


def broadcast(value, axis, root):
    mine = lax.axis_index(axis) == root
    return lax.psum(jnp.where(mine, value, jnp.zeros_like(value)), axis)


def make_table(samples):
    steps_n = jnp.arange(samples, dtype=jnp.int32)
    columns = []
    for freq in (samples // 16, samples // 8):
        phase = (freq * steps_n % samples).astype(jnp.float32) * jnp.float32(
            2.0 * math.pi / samples
        )
        columns.append(jnp.cos(phase))
        columns.append(-jnp.sin(phase))
    return jnp.stack(columns, axis=1) * jnp.float32(samples ** (-0.5))


def complex_step(cols, rows):
    left = cols.reshape(2, 2, cols.shape[1], cols.shape[2])
    right = rows.reshape(2, 2, rows.shape[1], rows.shape[2])
    part_re = jnp.einsum(
        "frk,fkc->frc", left[:, 0], right[:, 0], preferred_element_type=jnp.float32
    ) - jnp.einsum("frk,fkc->frc", left[:, 1], right[:, 1], preferred_element_type=jnp.float32)
    part_im = jnp.einsum(
        "frk,fkc->frc", left[:, 0], right[:, 1], preferred_element_type=jnp.float32
    ) + jnp.einsum("frk,fkc->frc", left[:, 1], right[:, 0], preferred_element_type=jnp.float32)
    return (part_re, part_im)


def body(data, traces, weight, dest, bins):
    n_rcv = lax.axis_size("rcv")
    n_shot = lax.axis_size("shot")
    devices = n_rcv * n_shot
    tr_dev = traces.shape[0]
    rec_dev = data.shape[1]
    shot_dev = data.shape[2]
    capacity = max(2, 2 * tr_dev // devices)
    spectra = jnp.dot(
        traces * weight[:, None], make_table(traces.shape[1]), precision=lax.Precision.HIGHEST
    )
    owner = dest[:, 0]
    one_hot = (owner[:, None] == jnp.arange(devices, dtype=jnp.int32)[None, :]).astype(jnp.int32)
    ranks = jnp.cumsum(one_hot, axis=0)
    position = jnp.take_along_axis(ranks, dest, axis=1)[:, 0] - 1
    slot_idx = owner * capacity + position
    empty_bin = rec_dev * shot_dev
    payload = jnp.zeros((4, devices * capacity), jnp.float32).at[:, slot_idx].set(spectra.T)
    bin_buffer = jnp.full((devices * capacity,), empty_bin, jnp.int32).at[slot_idx].set(bins)
    got_spectra = lax.all_to_all(
        payload.reshape(4, devices, capacity),
        ("rcv", "shot"),
        split_axis=1,
        concat_axis=1,
        tiled=True,
    )
    got_bins = lax.all_to_all(
        bin_buffer.reshape(devices, capacity),
        ("rcv", "shot"),
        split_axis=0,
        concat_axis=0,
        tiled=True,
    )
    got_spectra = got_spectra.reshape(4, devices * capacity)
    got_bins = got_bins.reshape(devices * capacity)
    full = (
        data.astype(jnp.float32)
        .reshape(4, rec_dev * shot_dev)
        .at[:, got_bins]
        .add(got_spectra, mode="drop")
    )
    binned = full.reshape(4, rec_dev, shot_dev).astype(jnp.bfloat16)
    panels = [step * n_shot // STEPS for step in range(STEPS)]
    roots = [panel * shot_dev // rec_dev for panel in panels]
    offsets = [panel * shot_dev % rec_dev for panel in panels]
    total_re = jnp.zeros((2, rec_dev, shot_dev), jnp.float32)
    total_im = jnp.zeros((2, rec_dev, shot_dev), jnp.float32)
    for step in range(STEPS):
        cols = broadcast(binned, "shot", panels[step])
        rows = broadcast(binned[:, offsets[step] : offsets[step] + shot_dev, :], "rcv", roots[step])
        part_re, part_im = complex_step(cols, rows)
        total_re = total_re + part_re
        total_im = total_im + part_im
    factor = jnp.float32((2 * STEPS * shot_dev) ** (-0.5))
    multiples = jnp.stack([total_re, total_im], axis=1).reshape(4, rec_dev, shot_dev) * factor
    return (binned, multiples)


def solution(mesh):
    placed = (
        P(None, "rcv", "shot"),
        P(("rcv", "shot"), None),
        P(("rcv", "shot")),
        P(("rcv", "shot"), None),
        P(("rcv", "shot")),
    )
    return jax.shard_map(
        body,
        mesh=mesh,
        in_specs=placed,
        out_specs=(P(None, "rcv", "shot"), P(None, "rcv", "shot")),
        check_vma=False,
    )
```

profile of v0, /device:TPU:8, one launch (start us, length us, event | category | flops | bytes accessed | tf_op | source)
XLA Modules:
  0.0 391.1 jit_solution(3974295950063348053)
XLA Ops:
  7.2 0.0 copy-start.10
  7.2 0.7 fusion.49
  7.9 0.8 copy.54
  8.7 0.2 fusion.26
  9.0 0.1 copy.56
  9.2 0.0 copy-start.9
  9.2 4.5 %gather_fusion = s32[512]{0:T(512)S(1)} fusion(s32[512,128]{0,1:T(8,128)S(1)} %bitcast.100, s32[512]{0:T(512)S(1)} %bitcast.99), kind=kCustom, calls=%fused_computation | custom fusion | bytes 8192 | tf_op jit(solution)/shard_map/jit(take_along_axis)/gather | solution.py:54
  13.8 2.6 scatter_custom_fusion
  16.4 0.7 all_to_all.9
  17.1 10.4 %all-to-all-start = ((s32[128,1,8]{2,1,0:T(1,128)}), s32[128,1,8]{2,1,0:T(1,128)S(1)}, u32[]{:S(2)}, u32[]{:S(2)}) async-start(s32[128,1,8]{2,1,0:T(1,128)} %bitcast.10), calls=%async_computation | async-start | bytes 131072 | tf_op jit(solution)/shard_map/all_to_all | solution.py:66
  27.6 0.5 sine_negate_fusion
  28.1 0.5 fusion.42
  28.6 5.3 %fusion.1 = f32[512,4]{1,0:T(8,128)S(1)} fusion(f32[512,2048]{1,0:T(8,128)} %param.6, f32[512]{0:T(512)S(1)} %copy-done.11, f32[2048,1]{0,1:T(1,128)S(1)} %get-tuple-element.28, f32[2048,1]{0,1:T(1,128)S(1)} %get-tuple-element.30, f32[2048,1]{0,1:T(1,128)S(1)} %get-tuple-element.29, f32[2048,1]{0,1:T(1,128)S(1)} %get-tuple-element.31), kind=kOutput, calls=%fused_computation.5 | convolution fusion | flops 51412992 | bytes 4237312 | tf_op jit(solution)/shard_map/dot_general | solution.py:48
  34.0 1.8 scatter_custom_fusion.1
  35.8 1.5 copy.59
  37.3 26.7 %copy.53 = f32[4,512,256]{0,2,1:T(8,128)} copy(bf16[4,512,256]{2,1,0:T(8,128)(2,1)S(1)} %copy-done.9) | data formatting | bytes 3145728 | tf_op jit(solution)/shard_map/reshape | solution.py:77
  64.0 9.8 %all-to-all-start.1 = ((f32[4,128,8]{2,0,1:T(4,128)}), f32[4,128,8]{2,0,1:T(4,128)S(1)}, u32[]{:S(2)}, u32[]{:S(2)}) async-start(f32[4,128,8]{2,0,1:T(4,128)} %copy.59), calls=%async_computation.1 | async-start | bytes 524288 | tf_op jit(solution)/shard_map/all_to_all | solution.py:59
  73.8 0.2 all-reduce.7.cloned.1.call-start
  74.0 0.5 broadcast.287
  74.5 0.8 reduce.3
  75.3 0.1 reshape.231
  75.5 3.8 sort
  79.2 5.1 %all-to-all-done.1 = f32[4,128,8]{2,0,1:T(4,128)S(1)} async-done(((f32[4,128,8]{2,0,1:T(4,128)}), f32[4,128,8]{2,0,1:T(4,128)S(1)}, u32[]{:S(2)}, u32[]{:S(2)}) %all-to-all-start.1) | async-done | bytes 16416 | tf_op jit(solution)/shard_map/all_to_all | solution.py:59
  84.4 0.2 reshape.269
  84.5 0.2 copy.61
  84.8 56.2 %scatter_custom_fusion.2 = f32[4,131072]{0,1:T(8,128)} fusion(f32[4,131072]{0,1:T(8,128)} %bitcast, s32[1024]{0:T(1024)S(1)} %get-tuple-element.10, f32[1024,4]{1,0:T(8,128)S(1)} %copy.61, s32[1024]{0:T(1024)S(1)} %broadcast_clamp_fusion), kind=kCustom, calls=%fused_computation.37 | custom fusion | flops 4096 | bytes 2097152 | tf_op jit(solution)/shard_map/scatter-add | solution.py:79
  140.9 32.3 %convert_element_type.47 = bf16[4,131072]{0,1:T(8,128)(2,1)} convert(f32[4,131072]{0,1:T(8,128)} %scatter_custom_fusion.2) | non-fusion elementwise | flops 524288 | bytes 3145728 | tf_op jit(solution)/shard_map/convert_element_type | solution.py:81
  173.2 25.2 %copy.76 = bf16[4,512,256]{2,1,0:T(8,128)(2,1)S(1)} copy(bf16[4,512,256]{0,2,1:T(8,128)(2,1)} %bitcast.98) | data formatting | bytes 2097152
  198.4 0.0 copy-start
  198.4 0.1 broadcast_select_fusion.4
  198.6 1.0 copy.65
  199.6 0.8 copy.68
  200.4 0.9 copy.71
  201.2 0.8 copy.74
  202.1 0.0 all-reduce.7.cloned.1.call-update
  202.1 0.0 all-reduce.5.cloned.1.call-start
  202.2 0.3 broadcast_select_fusion
  202.4 1.0 copy.63
  203.5 1.0 copy.67
  204.5 1.1 copy.70
  205.6 1.1 copy.73
  206.7 0.0 all-reduce.5.cloned.1.call-update
  206.7 59.2 %all-reduce.7.cloned.1.call-done = (bf16[2,2,256,256]{3,2,0,1:T(8,128)(2,1)}, bf16[2,2,256,256]{3,2,0,1:T(8,128)(2,1)}, bf16[2,2,256,256]{3,2,0,1:T(8,128)(2,1)}, bf16[2,2,256,256]{3,2,0,1:T(8,128)(2,1)}) async-done(((bf16[2,2,256,256]{3,2,0,1:T(8,128)(2,1)}, bf16[2,2,256,256]{3,2,0,1:T(8,128)(2,1)}, bf16[2,2,256,256]{3,2,0,1:T(8,128)(2,1)}, bf16[2,2,256,256]{3,2,0,1:T(8,128)(2,1)}), ...) | async-done | bytes 2097168 | tf_op jit(solution)/shard_map/psum | solution.py:13
  265.9 107.4 %all-reduce.5.cloned.1.call-done = (bf16[2,2,512,256]{3,2,0,1:T(8,128)(2,1)}, bf16[2,2,512,256]{3,2,0,1:T(8,128)(2,1)}, bf16[2,2,512,256]{3,2,0,1:T(8,128)(2,1)}, bf16[2,2,512,256]{3,2,0,1:T(8,128)(2,1)}) async-done(((bf16[2,2,512,256]{3,2,0,1:T(8,128)(2,1)}, bf16[2,2,512,256]{3,2,0,1:T(8,128)(2,1)}, bf16[2,2,512,256]{3,2,0,1:T(8,128)(2,1)}, bf16[2,2,512,256]{3,2,0,1:T(8,128)(2,1)}), ...) | async-done | bytes 4194320 | tf_op jit(solution)/shard_map/psum | solution.py:13
  373.3 1.5 fusion.23
  374.9 1.5 fusion.22
  376.4 1.4 fusion.21
  377.8 0.3 fusion.20
  378.2 0.3 fusion.19
  378.5 0.3 fusion.18
  378.8 0.3 fusion.17
  379.1 0.3 fusion.16
  379.4 0.3 convolution_subtract_fusion.3
  379.7 0.3 convolution_add_fusion.3
  380.0 0.3 fusion.11
  380.3 0.3 fusion.10
  380.6 0.6 copy-done.1
  381.2 0.1 copy-done.6
  381.3 0.3 fusion.9
  381.6 0.3 fusion.7
  381.9 0.3 fusion.6
  382.2 0.3 fusion.5
  382.5 0.2 maximum_multiply_fusion
  382.8 1.5 copy.75
  (34 shorter events, 0.2 us)
Async XLA Ops:
  7.2 6.6 %copy-start.10 = (s32[512,1]{0,1:T(1,128)S(1)}, s32[512,1]{0,1:T(1,128)}, u32[]{:S(2)}) copy-start(s32[512,1]{0,1:T(1,128)} %param.8) | copy-start | bytes 6148
  7.2 21.4 %copy-start.11 = (f32[512]{0:T(512)S(1)}, f32[512]{0:T(512)}, u32[]{:S(2)}) copy-start(f32[512]{0:T(512)} %param.7) | copy-start | bytes 6148
  9.2 28.1 %copy-start.9 = (bf16[4,512,256]{2,1,0:T(8,128)(2,1)S(1)}, bf16[4,512,256]{2,1,0:T(8,128)(2,1)}, u32[]{:S(2)}) copy-start(bf16[4,512,256]{2,1,0:T(8,128)(2,1)} %param.5) | copy-start | bytes 3145732
  17.1 46.9 %all-to-all-start = ((s32[128,1,8]{2,1,0:T(1,128)}), s32[128,1,8]{2,1,0:T(1,128)S(1)}, u32[]{:S(2)}, u32[]{:S(2)}) async-start(s32[128,1,8]{2,1,0:T(1,128)} %bitcast.10), calls=%async_computation | async-start | bytes 131072 | tf_op jit(solution)/shard_map/all_to_all | solution.py:66
  64.0 20.3 %all-to-all-start.1 = ((f32[4,128,8]{2,0,1:T(4,128)}), f32[4,128,8]{2,0,1:T(4,128)S(1)}, u32[]{:S(2)}, u32[]{:S(2)}) async-start(f32[4,128,8]{2,0,1:T(4,128)} %copy.59), calls=%async_computation.1 | async-start | bytes 524288 | tf_op jit(solution)/shard_map/all_to_all | solution.py:59
  73.8 192.1 %all-reduce.7.cloned.1.call-start = ((), (), s32[]{:S(2)}) async-start(), calls=%async_computation.3 | async-start | bytes 4194304 | tf_op jit(solution)/shard_map/psum | solution.py:13
  198.4 3.7 copy-start
  202.1 171.2 %all-reduce.5.cloned.1.call-start = ((), (), s32[]{:S(2)}) async-start(), calls=%async_computation.2 | async-start | bytes 8388608 | tf_op jit(solution)/shard_map/psum | solution.py:13
  265.9 111.9 %copy-start.7 = (bf16[2,2,256,256]{3,2,0,1:T(8,128)(2,1)S(1)}, bf16[2,2,256,256]{3,2,0,1:T(8,128)(2,1)}, u32[]{:S(2)}) copy-start(bf16[2,2,256,256]{3,2,0,1:T(8,128)(2,1)} %get-tuple-element.18) | copy-start | bytes 1572868
  265.9 112.2 %copy-start.8 = (bf16[2,2,256,256]{3,2,0,1:T(8,128)(2,1)S(1)}, bf16[2,2,256,256]{3,2,0,1:T(8,128)(2,1)}, u32[]{:S(2)}) copy-start(bf16[2,2,256,256]{3,2,0,1:T(8,128)(2,1)} %get-tuple-element.17) | copy-start | bytes 1572868
  373.3 4.5 %copy-start.2 = (bf16[2,2,512,256]{3,2,0,1:T(8,128)(2,1)S(1)}, bf16[2,2,512,256]{3,2,0,1:T(8,128)(2,1)}, u32[]{:S(2)}) copy-start(bf16[2,2,512,256]{3,2,0,1:T(8,128)(2,1)} %get-tuple-element.14) | copy-start | bytes 3145732
  373.3 4.8 %copy-start.3 = (bf16[2,2,512,256]{3,2,0,1:T(8,128)(2,1)S(1)}, bf16[2,2,512,256]{3,2,0,1:T(8,128)(2,1)}, u32[]{:S(2)}) copy-start(bf16[2,2,512,256]{3,2,0,1:T(8,128)(2,1)} %get-tuple-element.13) | copy-start | bytes 3145732
  374.9 3.9 copy-start.4
  374.9 3.9 copy-start.5
  380.0 1.2 copy-start.1
  380.0 1.3 copy-start.6
Sparse Core Ops, SparseCore 0:
  202.2 63.6 all-reduce.6
  270.1 103.2 all-reduce.4
where the time goes:
time: 393 us; the launch traced here: 391 us
  waiting for transfers between devices  172 us (44%)
  other arithmetic  95.6 us (24%)
  local copies, waits for them, and re-layouts  75 us (19%)
  starting transfers between devices  20.5 us (5%)
  between operations  14.5 us (4%)
  matrix products  13.6 us (3%)
    psum x2, waiting for transfers between devices, broadcast(): return lax.psum(jnp.where(mine, value, jnp.zeros_like(value)), axis)  167 us
    scatter-add x3, other arithmetic, body(): full = data.astype(jnp.float32).reshape(4, rec_dev * shot_dev).at[:, got_...  59.9 us
    convert_element_type x1, other arithmetic, body(): binned = full.reshape(4, rec_dev, shot_dev).astype(jnp.bfloat16)  32.3 us
    reshape x1, local copies, waits for them, and re-layouts, body(): full = data.astype(jnp.float32).reshape(4, rec_dev * shot_dev).at[:, got_...  26.7 us
    unnamed x27, local copies, waits for them, and re-layouts  26 us
    all_to_all x1, starting transfers between devices, body(): lax.all_to_all(bin_buffer.reshape(devices, capacity), ('rcv', 'shot'), sp...  10.4 us
    all_to_all x1, starting transfers between devices, body(): lax.all_to_all(payload.reshape(4, devices, capacity), ('rcv', 'shot'), sp...  9.76 us
  transfers between devices with their start and end apart: 4, of which 3 were waited for; matrix products, arithmetic and copies ran while one was open for 12% of the time, Pallas kernels for 0%

commit v1 on v0

v1 whole, which is shorter than its diff:
```python
import functools
import math

import jax
import jax.numpy as jnp
import numpy as np
from jax import lax
from jax.experimental import pallas as pl
from jax.experimental.pallas import tpu as pltpu
from jax.sharding import PartitionSpec as P

MESH = pl.DeviceIdType.MESH
SLOTS = 8
PERIOD = 128
CHUNKS = 16
STRETCH = 2

TREE = {
    (0, 0): ("b", "+y", "-y"),
    (3, 0): ("b",),
    (0, 1): ("f", "+y"),
    (1, 1): ("f", "-y"),
    (0, 3): ("b",),
    (3, 3): ("b",),
    (2, 3): ("-y",),
    (0, 2): ("f", "b"),
    (1, 2): ("+y",),
    (3, 2): ("-y",),
}
STEP = {"f": (1, 0), "b": (3, 0), "+y": (0, 1), "-y": (0, 3)}


def tree_depths():
    depths, front = {(0, 0): 0}, [(0, 0)]
    while front:
        at = front.pop(0)
        for way in TREE.get(at, ()):
            to = ((at[0] + STEP[way][0]) % 4, (at[1] + STEP[way][1]) % 4)
            assert to not in depths
            depths[to] = depths[at] + 1
            front.append(to)
    assert len(depths) == 16
    return depths


DEPTHS = tree_depths()


def table_t():
    n = np.arange(PERIOD)
    rows = []
    for freq in (128, 256):
        angle = (freq * n % 2048) * (2.0 * math.pi / 2048)
        rows += [np.cos(angle), -np.sin(angle)]
    rows = np.stack(rows) * 2048**-0.5
    return np.concatenate([rows, np.zeros((4, PERIOD))]).astype(np.float32)


def member(index, members):
    found = jnp.int32(0)
    for one in members:
        found = found + jnp.where(index == one, 1, 0)
    return found


def kernel(
    table, weight, dest, bins, data_hbm, traces_hbm, binned_hbm, mult_hbm,
    traces_v, data_v, send_a, recv_a, send_b, recv_b, rows_1h, cols_1h, cbuf, rbuf, binned_v, out_v,
    in_sem, a_send, a_recv, b_send, b_recv, c_send, c_recv, r_send, r_recv, out_sem,
):
    r = lax.axis_index("rcv")
    s = lax.axis_index("shot")
    x, y = s // 4, s % 4
    z, core = r // 2, r % 2
    f32, bf16 = jnp.float32, jnp.bfloat16

    trace_in = [
        pltpu.make_async_copy(traces_hbm.at[pl.ds(128 * i, 128)], traces_v.at[pl.ds(128 * i, 128)], in_sem.at[i])
        for i in range(4)
    ]
    data_in = pltpu.make_async_copy(data_hbm, data_v, in_sem.at[4])
    for one in trace_in:
        one.start()
    data_in.start()

    barrier = pltpu.get_barrier_semaphore()
    for k in range(1, 16):
        pl.semaphore_signal(barrier, inc=1, device_id=(r, lax.rem(s + k, 16)), device_id_type=MESH)
    for k in range(1, 8):
        pl.semaphore_signal(barrier, inc=1, device_id=(lax.rem(r + k, 8), s), device_id_type=MESH)

    owner = dest[...]
    owner = (owner & 15) * 8 + (owner >> 4)
    owner_1h = jnp.where(lax.broadcasted_iota(jnp.int32, (128, 512), 0) == owner, 1.0, 0.0)
    before = jnp.where(
        lax.broadcasted_iota(jnp.int32, (512, 512), 0) < lax.broadcasted_iota(jnp.int32, (512, 512), 1), 1.0, 0.0
    ).astype(bf16)
    owner_1h_b = owner_1h.astype(bf16)
    earlier = jnp.dot(owner_1h_b, before, preferred_element_type=f32)
    slot = jnp.sum(owner_1h * earlier, axis=0, keepdims=True)
    in_slot = lax.broadcasted_iota(jnp.int32, (SLOTS, 512), 0).astype(f32) == slot

    spectra = []
    for i in range(4):
        trace_in[i].wait()
        folded = traces_v[pl.ds(128 * i, 128), 0:PERIOD]
        for b in range(1, 16):
            folded = folded + traces_v[pl.ds(128 * i, 128), PERIOD * b : PERIOD * (b + 1)]
        spectra.append(
            lax.dot_general(
                table[...], folded, (((1,), (1,)), ((), ())),
                precision=lax.Precision.HIGHEST, preferred_element_type=f32,
            )
        )
    spectra = jnp.concatenate(spectra, axis=1)[0:4] * weight[...]
    high = spectra.astype(bf16).astype(f32)
    low = (spectra - high).astype(bf16).astype(f32)
    place = bins[...]
    words = [high[w : w + 1] for w in range(4)] + [low[w : w + 1] for w in range(4)]
    words += [(place >> 16).astype(f32), ((place >> 8) & 255).astype(f32), (place & 255).astype(f32)]
    listing = [jnp.where(in_slot, word, 0.0) for word in words]
    listing.append(jnp.zeros((128 - SLOTS * len(words), 512), f32))
    listing = jnp.concatenate(listing, axis=0).astype(bf16)
    send_a[...] = lax.dot_general(owner_1h_b, listing, (((1,), (1,)), ((), ())), preferred_element_type=f32)

    pl.semaphore_wait(barrier, 22)

    def copy_a(k):
        to = lax.rem(s + k, 16)
        return pltpu.make_async_remote_copy(
            src_ref=send_a.at[pl.ds(to * 8, 8)], dst_ref=recv_a.at[pl.ds(s * 8, 8)],
            send_sem=a_send.at[k - 1], recv_sem=a_recv.at[k - 1],
            device_id=(r, to), device_id_type=MESH,
        )

    def copy_b(k):
        to = lax.rem(r + k, 8)
        return pltpu.make_async_remote_copy(
            src_ref=send_b.at[pl.ds(to * 16, 16)], dst_ref=recv_b.at[pl.ds(r * 16, 16)],
            send_sem=b_send.at[k - 1], recv_sem=b_recv.at[k - 1],
            device_id=(to, s), device_id_type=MESH,
        )

    for k in range(1, 16):
        copy_a(k).start()
    own = pl.ds(pl.multiple_of(s * 8, 8), 8)
    recv_a[own] = send_a[own]
    for k in range(1, 16):
        copy_a(k).wait()
    for k in range(8):
        send_b[16 * k : 16 * (k + 1)] = recv_a[pl.ds(k, 16, stride=8)]
    for k in range(1, 8):
        copy_b(k).start()
    own = pl.ds(pl.multiple_of(r * 16, 16), 16)
    recv_b[own] = send_b[own]
    for k in range(1, 8):
        copy_b(k).wait()

    got = recv_b[...]
    got_t = jnp.transpose(got)
    for slot_at in range(SLOTS):
        k_at = pl.ds(128 * slot_at, 128)
        row = got_t[64 + slot_at : 65 + slot_at] * 256.0 + got_t[72 + slot_at : 73 + slot_at]
        rows_1h[:, k_at] = jnp.where(
            lax.broadcasted_iota(jnp.int32, (512, 128), 0).astype(f32) == row, 1.0, 0.0
        ).astype(bf16)
        column = got[:, 80 + slot_at : 81 + slot_at]
        at_column = lax.broadcasted_iota(jnp.int32, (128, 256), 1).astype(f32) == column
        for w in range(8):
            value = got[:, 8 * w + slot_at : 8 * w + slot_at + 1]
            cols_1h[w, k_at] = jnp.where(at_column, value, 0.0).astype(bf16)
    data_in.wait()
    for w in range(4):
        added = jnp.dot(rows_1h[...], cols_1h[w], preferred_element_type=f32)
        added = added + jnp.dot(rows_1h[...], cols_1h[w + 4], preferred_element_type=f32)
        binned_v[w] = (data_v[w].astype(f32) + added).astype(bf16)

    binned_out = pltpu.make_async_copy(binned_v, binned_hbm, out_sem.at[0])
    binned_out.start()

    @pl.when(y == 0)
    def _():
        cbuf[x] = binned_v[...]

    @pl.when(core == 0)
    def _():
        rbuf[z] = binned_v[:, 0:256, :]

    streams = []
    for p in range(4):
        for v in range(2):
            dx = lax.rem(x - p + 4, 4) if v == 0 else lax.rem(p - x + 4, 4)
            at = dx * 4 + y
            depth = jnp.int32(0)
            for node, value in DEPTHS.items():
                depth = depth + jnp.where(at == node[0] * 4 + node[1], value, 0)
            ways = {}
            for way in STEP:
                ways[way] = member(at, [n[0] * 4 + n[1] for n in TREE if way in TREE[n]])
            streams.append((p, v, depth, ways))
    up, down = lax.rem(x + 1, 4), lax.rem(x + 3, 4)

    def target(way, v):
        if way == "+y":
            return (r, x * 4 + lax.rem(y + 1, 4))
        if way == "-y":
            return (r, x * 4 + lax.rem(y + 3, 4))
        return (r, (up if (way == "f") == (v == 0) else down) * 4 + y)

    way_index = {way: i for i, way in enumerate(STEP)}

    def column_copy(p, v, j, way):
        comp = (j // 8) * 2 + lax.rem(j, 2)
        start = v * 256 + lax.rem(j // 2, 4) * 64
        ref = cbuf.at[p, comp, pl.ds(pl.multiple_of(start, 64), 64)]
        return pltpu.make_async_remote_copy(
            src_ref=ref, dst_ref=ref, send_sem=c_send.at[2 * p + v, way_index[way]],
            recv_sem=c_recv.at[2 * p + v, j], device_id=target(way, v), device_id_type=MESH,
        )

    z_up = (lax.rem(z + 1, 4) * 2 + core, s)
    z_down = (lax.rem(z + 3, 4) * 2 + core, s)
    z_core = (z * 2 + 1 - core, s)

    def row_copy(p, k, way):
        ref = rbuf.at[p, k]
        return pltpu.make_async_remote_copy(
            src_ref=ref, dst_ref=ref, send_sem=r_send.at[p, way], recv_sem=r_recv.at[p, k],
            device_id=(z_up, z_down, z_core)[way], device_id_type=MESH,
        )

    row_roles = []
    for p in range(4):
        dz = lax.rem(z - p + 4, 4)
        row_roles.append((p, dz, jnp.where(dz == 3, 1, dz) + core))

    @pl.loop(0, CHUNKS + 4 * STRETCH)
    def _(t):
        for p, v, depth, ways in streams:
            j = t - depth * STRETCH

            @pl.when((j >= 0) & (j < CHUNKS))
            def _():
                @pl.when(depth > 0)
                def _():
                    column_copy(p, v, j, "f").wait_recv()

                for way in STEP:
                    @pl.when(ways[way] == 1)
                    def _():
                        column_copy(p, v, j, way).start()

        for p, dz, depth in row_roles:
            k = t // 2 - depth

            @pl.when((lax.rem(t, 2) == 0) & (k >= 0) & (k < 4))
            def _():
                @pl.when(depth > 0)
                def _():
                    row_copy(p, k, 0).wait_recv()

                @pl.when(core == 0)
                def _():
                    row_copy(p, k, 2).start()

                    @pl.when((dz == 0) | ((dz == 1) & (k < 2)))
                    def _():
                        row_copy(p, k, 0).start()

                    @pl.when((dz == 0) | ((dz == 3) & (k >= 2)))
                    def _():
                        row_copy(p, k, 1).start()

    factor = 2048**-0.5
    for f in range(2):
        @pl.loop(0, 4)
        def _(i):
            at = pl.ds(pl.multiple_of(i * 128, 128), 128)
            re = jnp.zeros((128, 256), f32)
            im = jnp.zeros((128, 256), f32)
            for p in range(4):
                c_re, c_im = cbuf[p, 2 * f, at], cbuf[p, 2 * f + 1, at]
                r_re, r_im = rbuf[p, 2 * f], rbuf[p, 2 * f + 1]
                re = re + jnp.dot(c_re, r_re, preferred_element_type=f32)
                re = re - jnp.dot(c_im, r_im, preferred_element_type=f32)
                im = im + jnp.dot(c_re, r_im, preferred_element_type=f32)
                im = im + jnp.dot(c_im, r_re, preferred_element_type=f32)
            out_v[2 * f, at] = re * factor
            out_v[2 * f + 1, at] = im * factor

        pltpu.make_async_copy(out_v.at[pl.ds(2 * f, 2)], mult_hbm.at[pl.ds(2 * f, 2)], out_sem.at[1 + f]).start()

    for p, v, depth, ways in streams:
        for way in STEP:
            @pl.when(ways[way] == 1)
            def _():
                half = cbuf.at[p, :, pl.ds(v * 256, 256)]
                pltpu.make_async_remote_copy(
                    src_ref=half, dst_ref=half, send_sem=c_send.at[2 * p + v, way_index[way]],
                    recv_sem=c_recv.at[2 * p + v, 0], device_id=target(way, v), device_id_type=MESH,
                ).wait_send()

    def row_wait(p, ref, way):
        pltpu.make_async_remote_copy(
            src_ref=ref, dst_ref=ref, send_sem=r_send.at[p, way], recv_sem=r_recv.at[p, 0],
            device_id=(z_up, z_down, z_core)[way], device_id_type=MESH,
        ).wait_send()

    for p, dz, depth in row_roles:
        @pl.when(core == 0)
        def _():
            row_wait(p, rbuf.at[p], 2)

            @pl.when(dz == 0)
            def _():
                row_wait(p, rbuf.at[p], 0)
                row_wait(p, rbuf.at[p], 1)

            @pl.when(dz == 1)
            def _():
                row_wait(p, rbuf.at[p, pl.ds(0, 2)], 0)

            @pl.when(dz == 3)
            def _():
                row_wait(p, rbuf.at[p, pl.ds(2, 2)], 1)

    binned_out.wait()
    for f in range(2):
        pltpu.make_async_copy(out_v.at[pl.ds(2 * f, 2)], mult_hbm.at[pl.ds(2 * f, 2)], out_sem.at[1 + f]).wait()


def body(data, traces, weight, dest, bins):
    f32, bf16 = jnp.float32, jnp.bfloat16
    vmem = pl.BlockSpec(memory_space=pltpu.VMEM)
    hbm = pl.BlockSpec(memory_space=pl.ANY)
    dma = pltpu.SemaphoreType.DMA
    return pl.pallas_call(
        kernel,
        out_shape=(
            jax.ShapeDtypeStruct((4, 512, 256), bf16),
            jax.ShapeDtypeStruct((4, 512, 256), f32),
        ),
        in_specs=[vmem, vmem, vmem, vmem, hbm, hbm],
        out_specs=(hbm, hbm),
        scratch_shapes=[
            pltpu.VMEM((512, 2048), f32),
            pltpu.VMEM((4, 512, 256), bf16),
            pltpu.VMEM((128, 128), f32),
            pltpu.VMEM((128, 128), f32),
            pltpu.VMEM((128, 128), f32),
            pltpu.VMEM((128, 128), f32),
            pltpu.VMEM((512, 1024), bf16),
            pltpu.VMEM((8, 1024, 256), bf16),
            pltpu.VMEM((4, 4, 512, 256), bf16),
            pltpu.VMEM((4, 4, 256, 256), bf16),
            pltpu.VMEM((4, 512, 256), bf16),
            pltpu.VMEM((4, 512, 256), f32),
            dma((5,)),
            dma((15,)),
            dma((15,)),
            dma((7,)),
            dma((7,)),
            dma((8, 4)),
            dma((8, CHUNKS)),
            dma((4, 3)),
            dma((4, 4)),
            dma((3,)),
        ],
        compiler_params=pltpu.CompilerParams(
            collective_id=0, has_side_effects=True, vmem_limit_bytes=40 * 2**20
        ),
        cost_estimate=pl.CostEstimate(flops=5 * 10**9, bytes_accessed=9 * 2**20, transcendentals=0),
    )(
        jnp.asarray(table_t()),
        weight.reshape(1, 512),
        dest.reshape(1, 512),
        bins.reshape(1, 512),
        data,
        traces,
    )


def solution(mesh):
    placed = (
        P(None, "rcv", "shot"),
        P(("rcv", "shot"), None),
        P(("rcv", "shot")),
        P(("rcv", "shot"), None),
        P(("rcv", "shot")),
    )
    return jax.shard_map(
        body,
        mesh=mesh,
        in_specs=placed,
        out_specs=(P(None, "rcv", "shot"), P(None, "rcv", "shot")),
        check_vma=False,
    )
```

time: 393 us -> 79 us (0.20)
  waiting for transfers between devices: 172 us -> 0 us
  other arithmetic: 95.6 us -> 0 us
  Pallas kernels: 0 us -> 69.6 us
  local copies, waits for them, and re-layouts: 75 us -> 8.43 us
  starting transfers between devices: 20.5 us -> 0 us
  between operations: 14.5 us -> 0.65 us
  matrix products: 13.6 us -> 0 us
    psum x2 -> x0, waiting for transfers between devices: 167 us -> none  [broadcast(): return lax.psum(jnp.where(mine, value, jnp.zeros_like(value)), axis)]
    pallas_call x0 -> x1, Pallas kernels: none -> 69.6 us  [body(): pl.pallas_call(kernel, out_shape=(jax.ShapeDtypeStruct((4, 512, 256), bf1...]
    scatter-add x3 -> x0, other arithmetic: 59.9 us -> none  [body(): full = data.astype(jnp.float32).reshape(4, rec_dev * shot_dev).at[:, got_...]
    reshape x13 -> x0, local copies, waits for them, and re-layouts: 36.4 us -> none  [the longest x1 26.7 us: body(): full = data.astype(jnp.float32).reshape(4, rec_dev * shot_dev).at[:, got_...]
    convert_element_type x1 -> x0, other arithmetic: 32.3 us -> none  [body(): binned = full.reshape(4, rec_dev, shot_dev).astype(jnp.bfloat16)]
    all_to_all x2 -> x0, starting transfers between devices: 20.2 us -> none  [the longest x1 10.4 us: body(): lax.all_to_all(bin_buffer.reshape(devices, capacity), ('rcv', 'shot'), sp...]
    unnamed x27 -> x14, local copies, waits for them, and re-layouts: 26 us -> 8.43 us
    dot_general x17 -> x0, matrix products: 13.6 us -> none  [the longest x1 5.34 us: body(): jnp.dot(traces * weight[:, None], make_table(traces.shape[1]), precision=...]
  transfers between devices with their start and end apart: 4 -> 0, of which waited for: 3 -> 0; matrix products, arithmetic and copies ran while one was open for 12% -> 0% of each run, Pallas kernels for 0% -> 0%
where the time goes in v1:
time: 79 us; the launch traced here: 78.7 us
  Pallas kernels  69.6 us (88%)
  local copies, waits for them, and re-layouts  8.43 us (11%)
    pallas_call x1, Pallas kernels, body(): pl.pallas_call(kernel, out_shape=(jax.ShapeDtypeStruct((4, 512, 256), bf1...  69.6 us
    unnamed x14, local copies, waits for them, and re-layouts  8.43 us

profile of v1, /device:TPU:8, one launch (start us, length us, event | category | flops | bytes accessed | tf_op | source)
XLA Modules:
  0.0 78.7 jit_solution(8608871705276839465)
XLA Ops:
  0.6 0.0 copy-start
  0.6 2.2 %copy-done = f32[512,2048]{1,0:T(8,128)S(1)} copy-done((f32[512,2048]{1,0:T(8,128)S(1)}, f32[512,2048]{1,0:T(8,128)}, u32[]{:S(2)}) %copy-start) | copy-done | bytes 4194328
  2.8 0.0 copy-start.1
  2.8 1.2 %copy-done.1 = bf16[4,512,256]{2,1,0:T(8,128)(2,1)S(1)} copy-done((bf16[4,512,256]{2,1,0:T(8,128)(2,1)S(1)}, bf16[4,512,256]{2,1,0:T(8,128)(2,1)}, u32[]{:S(2)}) %copy-start.1) | copy-done | bytes 1048600
  4.0 0.0 copy-start.2
  4.0 0.7 copy-done.2
  4.7 0.0 copy-start.3
  4.7 0.7 copy-done.3
  5.4 0.0 copy-start.4
  5.4 0.7 copy-done.4
  6.1 0.0 copy-start.5
  6.1 0.7 copy-done.5
  6.8 69.6 %shard_map.77 = (bf16[4,512,256]{2,1,0:T(8,128)(2,1)S(1)}, f32[4,512,256]{2,1,0:T(8,128)S(1)}) custom-call(f32[8,128]{1,0:T(8,128)S(1)} %copy-done.5, f32[1,512]{1,0:T(1,128)S(1)} %bitcast.3, s32[1,512]{1,0:T(1,128)S(1)} %bitcast.4, s32[1,512]{1,0:T(1,128)S(1)} %bitcast.5, bf16[4,512,256]{2,1,0:T(8,128)(2,1)S(1)} %copy-done.1, f32[512,2048]{1,0:T(8,128)S(1)} %copy-done), custom_call_target="tpu_custom_call" | custom-call | flops 5000000000 | bytes 9437184 | tf_op jit(solution)/shard_map/pallas_call | solution.py:337
  76.4 1.0 %copy.10 = bf16[4,512,256]{2,1,0:T(8,128)(2,1)} copy(bf16[4,512,256]{2,1,0:T(8,128)(2,1)S(1)} %get-tuple-element.4) | data formatting | bytes 2097152
  77.4 1.3 %copy.11 = f32[4,512,256]{2,1,0:T(8,128)} copy(f32[4,512,256]{2,1,0:T(8,128)S(1)} %get-tuple-element.5) | data formatting | bytes 4194304
Async XLA Ops:
  0.6 2.2 %copy-start = (f32[512,2048]{1,0:T(8,128)S(1)}, f32[512,2048]{1,0:T(8,128)}, u32[]{:S(2)}) copy-start(f32[512,2048]{1,0:T(8,128)} %traces_hbm.1) | copy-start | bytes 12582916
  2.8 1.2 %copy-start.1 = (bf16[4,512,256]{2,1,0:T(8,128)(2,1)S(1)}, bf16[4,512,256]{2,1,0:T(8,128)(2,1)}, u32[]{:S(2)}) copy-start(bf16[4,512,256]{2,1,0:T(8,128)(2,1)} %data_hbm.1) | copy-start | bytes 3145732
  4.0 0.7 copy-start.2
  4.7 0.7 copy-start.3
  5.4 0.7 copy-start.4
  6.1 0.7 copy-start.5

commit v2 on v1

--- a/solution.py
+++ b/solution.py
@@ -13,7 +13,7 @@
 SLOTS = 8
 PERIOD = 128
 CHUNKS = 16
-STRETCH = 2
+STRETCH = 3
 
 TREE = {
     (0, 0): ("b", "+y", "-y"),
@@ -64,9 +64,11 @@
 
 
 def kernel(
-    table, weight, dest, bins, data_hbm, traces_hbm, binned_hbm, mult_hbm,
-    traces_v, data_v, send_a, recv_a, send_b, recv_b, rows_1h, cols_1h, cbuf, rbuf, binned_v, out_v,
-    in_sem, a_send, a_recv, b_send, b_recv, c_send, c_recv, r_send, r_recv, out_sem,
+    table_hbm, weight_hbm, dest_hbm, bins_hbm, data_hbm, traces_hbm, binned_hbm, mult_hbm,
+    table, weight, dest, bins, traces_v, data_v, send_a, recv_a, send_b, recv_b, rows_1h, cols_1h,
+    cbuf, rbuf, rbuf_0, corr_c, corr_r, corr_own, delta, binned_v, out_v,
+    in_sem, a_send, a_recv, b_send, b_recv, c_send, c_recv, r_send, r_recv,
+    cc_send, cc_recv, cr_send, cr_recv, out_sem,
 ):
     r = lax.axis_index("rcv")
     s = lax.axis_index("shot")
@@ -74,11 +76,17 @@
     z, core = r // 2, r % 2
     f32, bf16 = jnp.float32, jnp.bfloat16
 
+    small_in = [
+        pltpu.make_async_copy(one, to, in_sem.at[5 + i])
+        for i, (one, to) in enumerate(((dest_hbm, dest), (table_hbm, table), (weight_hbm, weight), (bins_hbm, bins)))
+    ]
     trace_in = [
         pltpu.make_async_copy(traces_hbm.at[pl.ds(128 * i, 128)], traces_v.at[pl.ds(128 * i, 128)], in_sem.at[i])
         for i in range(4)
     ]
     data_in = pltpu.make_async_copy(data_hbm, data_v, in_sem.at[4])
+    for one in small_in:
+        one.start()
     for one in trace_in:
         one.start()
     data_in.start()
@@ -89,6 +97,8 @@
     for k in range(1, 8):
         pl.semaphore_signal(barrier, inc=1, device_id=(lax.rem(r + k, 8), s), device_id_type=MESH)
 
+    for one in small_in:
+        one.wait()
     owner = dest[...]
     owner = (owner & 15) * 8 + (owner >> 4)
     owner_1h = jnp.where(lax.broadcasted_iota(jnp.int32, (128, 512), 0) == owner, 1.0, 0.0)
@@ -123,68 +133,15 @@
     listing = jnp.concatenate(listing, axis=0).astype(bf16)
     send_a[...] = lax.dot_general(owner_1h_b, listing, (((1,), (1,)), ((), ())), preferred_element_type=f32)
 
-    pl.semaphore_wait(barrier, 22)
-
-    def copy_a(k):
-        to = lax.rem(s + k, 16)
-        return pltpu.make_async_remote_copy(
-            src_ref=send_a.at[pl.ds(to * 8, 8)], dst_ref=recv_a.at[pl.ds(s * 8, 8)],
-            send_sem=a_send.at[k - 1], recv_sem=a_recv.at[k - 1],
-            device_id=(r, to), device_id_type=MESH,
-        )
-
-    def copy_b(k):
-        to = lax.rem(r + k, 8)
-        return pltpu.make_async_remote_copy(
-            src_ref=send_b.at[pl.ds(to * 16, 16)], dst_ref=recv_b.at[pl.ds(r * 16, 16)],
-            send_sem=b_send.at[k - 1], recv_sem=b_recv.at[k - 1],
-            device_id=(to, s), device_id_type=MESH,
-        )
-
-    for k in range(1, 16):
-        copy_a(k).start()
-    own = pl.ds(pl.multiple_of(s * 8, 8), 8)
-    recv_a[own] = send_a[own]
-    for k in range(1, 16):
-        copy_a(k).wait()
-    for k in range(8):
-        send_b[16 * k : 16 * (k + 1)] = recv_a[pl.ds(k, 16, stride=8)]
-    for k in range(1, 8):
-        copy_b(k).start()
-    own = pl.ds(pl.multiple_of(r * 16, 16), 16)
-    recv_b[own] = send_b[own]
-    for k in range(1, 8):
-        copy_b(k).wait()
-
-    got = recv_b[...]
-    got_t = jnp.transpose(got)
-    for slot_at in range(SLOTS):
-        k_at = pl.ds(128 * slot_at, 128)
-        row = got_t[64 + slot_at : 65 + slot_at] * 256.0 + got_t[72 + slot_at : 73 + slot_at]
-        rows_1h[:, k_at] = jnp.where(
-            lax.broadcasted_iota(jnp.int32, (512, 128), 0).astype(f32) == row, 1.0, 0.0
-        ).astype(bf16)
-        column = got[:, 80 + slot_at : 81 + slot_at]
-        at_column = lax.broadcasted_iota(jnp.int32, (128, 256), 1).astype(f32) == column
-        for w in range(8):
-            value = got[:, 8 * w + slot_at : 8 * w + slot_at + 1]
-            cols_1h[w, k_at] = jnp.where(at_column, value, 0.0).astype(bf16)
     data_in.wait()
-    for w in range(4):
-        added = jnp.dot(rows_1h[...], cols_1h[w], preferred_element_type=f32)
-        added = added + jnp.dot(rows_1h[...], cols_1h[w + 4], preferred_element_type=f32)
-        binned_v[w] = (data_v[w].astype(f32) + added).astype(bf16)
-
-    binned_out = pltpu.make_async_copy(binned_v, binned_hbm, out_sem.at[0])
-    binned_out.start()
 
     @pl.when(y == 0)
     def _():
-        cbuf[x] = binned_v[...]
+        cbuf[x, 0:2] = data_v[0:2]
 
     @pl.when(core == 0)
     def _():
-        rbuf[z] = binned_v[:, 0:256, :]
+        rbuf[z, 0:2] = data_v[0:2, 0:256]
 
     streams = []
     for p in range(4):
@@ -223,7 +180,7 @@
     z_core = (z * 2 + 1 - core, s)
 
     def row_copy(p, k, way):
-        ref = rbuf.at[p, k]
+        ref = rbuf.at[p, k // 2, pl.ds(pl.multiple_of(lax.rem(k, 2) * 128, 128), 128)]
         return pltpu.make_async_remote_copy(
             src_ref=ref, dst_ref=ref, send_sem=r_send.at[p, way], recv_sem=r_recv.at[p, k],
             device_id=(z_up, z_down, z_core)[way], device_id_type=MESH,
@@ -234,8 +191,7 @@
         dz = lax.rem(z - p + 4, 4)
         row_roles.append((p, dz, jnp.where(dz == 3, 1, dz) + core))
 
-    @pl.loop(0, CHUNKS + 4 * STRETCH)
-    def _(t):
+    def step(t):
         for p, v, depth, ways in streams:
             j = t - depth * STRETCH
 
@@ -251,9 +207,10 @@
                         column_copy(p, v, j, way).start()
 
         for p, dz, depth in row_roles:
-            k = t // 2 - depth
-
-            @pl.when((lax.rem(t, 2) == 0) & (k >= 0) & (k < 4))
+            at = t - depth * STRETCH
+            k = jnp.where(at >= 8, at - 4, at)
+
+            @pl.when((at >= 0) & (k < 8) & ((at < 4) | (at >= 8)))
             def _():
                 @pl.when(depth > 0)
                 def _():
@@ -263,32 +220,202 @@
                 def _():
                     row_copy(p, k, 2).start()
 
-                    @pl.when((dz == 0) | ((dz == 1) & (k < 2)))
+                    @pl.when((dz == 0) | ((dz == 1) & (lax.rem(k, 2) == 0)))
                     def _():
                         row_copy(p, k, 0).start()
 
-                    @pl.when((dz == 0) | ((dz == 3) & (k >= 2)))
+                    @pl.when((dz == 0) | ((dz == 3) & (lax.rem(k, 2) == 1)))
                     def _():
                         row_copy(p, k, 1).start()
 
+    def steps(first, last):
+        @pl.loop(first, last)
+        def _(t):
+            step(t)
+
+    def copy_a(k):
+        to = lax.rem(s + k, 16)
+        return pltpu.make_async_remote_copy(
+            src_ref=send_a.at[pl.ds(to * 8, 8)], dst_ref=recv_a.at[pl.ds(s * 8, 8)],
+            send_sem=a_send.at[k - 1], recv_sem=a_recv.at[k - 1],
+            device_id=(r, to), device_id_type=MESH,
+        )
+
+    def copy_b(k):
+        to = lax.rem(r + k, 8)
+        return pltpu.make_async_remote_copy(
+            src_ref=send_b.at[pl.ds(to * 16, 16)], dst_ref=recv_b.at[pl.ds(r * 16, 16)],
+            send_sem=b_send.at[k - 1], recv_sem=b_recv.at[k - 1],
+            device_id=(to, s), device_id_type=MESH,
+        )
+
+    def corr_column(k):
+        return pltpu.make_async_remote_copy(
+            src_ref=corr_own, dst_ref=corr_c.at[x], send_sem=cc_send.at[k - 1], recv_sem=cc_recv.at[x],
+            device_id=(r, lax.rem(s + k, 16)), device_id_type=MESH,
+        )
+
+    def corr_row(k):
+        return pltpu.make_async_remote_copy(
+            src_ref=corr_own, dst_ref=corr_r.at[z], send_sem=cr_send.at[k - 1], recv_sem=cr_recv.at[z],
+            device_id=(lax.rem(r + k, 8), s), device_id_type=MESH,
+        )
+
+    def build_rows(got_t, count):
+        for slot_at in range(SLOTS):
+            high_row = got_t[64 + slot_at : 65 + slot_at]
+            low_row = got_t[72 + slot_at : 73 + slot_at]
+            for h in range(count // 256):
+                row = jnp.where(high_row == float(h), low_row, -1.0).astype(bf16)
+                rows_1h[256 * h : 256 * (h + 1), 128 * slot_at : 128 * (slot_at + 1)] = jnp.where(
+                    iota_row == row, jnp.bfloat16(1), jnp.bfloat16(0)
+                )
+
+    def build_cols(got, f):
+        for slot_at in range(SLOTS):
+            column = got[:, 80 + slot_at : 81 + slot_at]
+            at_column = iota_col == column
+            for i, w in enumerate((2 * f, 2 * f + 1, 4 + 2 * f, 5 + 2 * f)):
+                value = got[:, 8 * w + slot_at : 8 * w + slot_at + 1]
+                cols_1h[i, 128 * slot_at : 128 * (slot_at + 1)] = jnp.where(at_column, value, jnp.bfloat16(0))
+
+    def added(i, count):
+        total = jnp.dot(rows_1h[0:count], cols_1h[i], preferred_element_type=f32)
+        return total + jnp.dot(rows_1h[0:count], cols_1h[i + 2], preferred_element_type=f32)
+
+    iota_row = lax.broadcasted_iota(jnp.int32, (256, 128), 0).astype(f32).astype(bf16)
+    iota_col = lax.broadcasted_iota(jnp.int32, (128, 256), 1).astype(f32).astype(bf16)
+
+    pl.semaphore_wait(barrier, 22)
+
+    for k in range(1, 16):
+        copy_a(k).start()
+    own = pl.ds(pl.multiple_of(s * 8, 8), 8)
+    recv_a[own] = send_a[own]
+    steps(0, 4)
+    for k in range(1, 16):
+        copy_a(k).wait()
+    for k in range(8):
+        send_b[16 * k : 16 * (k + 1)] = recv_a[pl.ds(k, 16, stride=8)]
+    for k in range(1, 8):
+        copy_b(k).start()
+    own = pl.ds(pl.multiple_of(r * 16, 16), 16)
+    recv_b[own] = send_b[own]
+    steps(4, 7)
+    for k in range(1, 8):
+        copy_b(k).wait()
+    corr_own[...] = recv_b[...].astype(bf16)
+
+    @pl.when(y == 0)
+    def _():
+        for k in range(1, 16):
+            corr_column(k).start()
+        corr_c[x] = corr_own[...]
+
+    @pl.when(core == 0)
+    def _():
+        for k in range(1, 8):
+            corr_row(k).start()
+        corr_r[z] = corr_own[...]
+
+    steps(7, 8)
+
+    build_rows(jnp.transpose(recv_b[...]), 512)
+    for f in (1, 0):
+        build_cols(corr_own[...], f)
+        for i in range(2):
+            binned_v[2 * f + i] = (data_v[2 * f + i].astype(f32) + added(i, 512)).astype(bf16)
+        if f == 1:
+            @pl.when(y == 0)
+            def _():
+                cbuf[x, 2:4] = binned_v[2:4]
+
+            @pl.when(core == 0)
+            def _():
+                rbuf[z, 2:4] = binned_v[2:4, 0:256]
+
+            steps(8, 9)
+    binned_out = pltpu.make_async_copy(binned_v, binned_hbm, out_sem.at[0])
+    binned_out.start()
+    steps(9, 12)
+
+    for p in range(4):
+        @pl.when((y != 0) | (x != p))
+        def _():
+            pltpu.make_async_remote_copy(
+                src_ref=corr_own, dst_ref=corr_c.at[p], send_sem=cc_send.at[0], recv_sem=cc_recv.at[p],
+                device_id=(r, lax.rem(s + 1, 16)), device_id_type=MESH,
+            ).wait_recv()
+
+        @pl.when((core != 0) | (z != p))
+        def _():
+            pltpu.make_async_remote_copy(
+                src_ref=corr_own, dst_ref=corr_r.at[p], send_sem=cr_send.at[0], recv_sem=cr_recv.at[p],
+                device_id=(lax.rem(r + 1, 8), s), device_id_type=MESH,
+            ).wait_recv()
+
+    @pl.loop(12, 16)
+    def _(t):
+        step(t)
+        p = t - 12
+        got = corr_r[p]
+        build_rows(jnp.transpose(got.astype(f32)), 256)
+        build_cols(got, 0)
+        for i in range(2):
+            rbuf_0[p, i] = (rbuf[p, i].astype(f32) + added(i, 256)).astype(bf16)
+
+    @pl.loop(16, 20)
+    def _(t):
+        step(t)
+        p = t - 16
+        got = corr_c[p]
+        build_rows(jnp.transpose(got.astype(f32)), 512)
+        build_cols(got, 0)
+        for i in range(2):
+            delta[p, i] = added(i, 512)
+
     factor = 2048**-0.5
-    for f in range(2):
-        @pl.loop(0, 4)
-        def _(i):
-            at = pl.ds(pl.multiple_of(i * 128, 128), 128)
-            re = jnp.zeros((128, 256), f32)
-            im = jnp.zeros((128, 256), f32)
-            for p in range(4):
-                c_re, c_im = cbuf[p, 2 * f, at], cbuf[p, 2 * f + 1, at]
-                r_re, r_im = rbuf[p, 2 * f], rbuf[p, 2 * f + 1]
-                re = re + jnp.dot(c_re, r_re, preferred_element_type=f32)
-                re = re - jnp.dot(c_im, r_im, preferred_element_type=f32)
-                im = im + jnp.dot(c_re, r_im, preferred_element_type=f32)
-                im = im + jnp.dot(c_im, r_re, preferred_element_type=f32)
-            out_v[2 * f, at] = re * factor
-            out_v[2 * f + 1, at] = im * factor
-
-        pltpu.make_async_copy(out_v.at[pl.ds(2 * f, 2)], mult_hbm.at[pl.ds(2 * f, 2)], out_sem.at[1 + f]).start()
+
+    def product(f, c_re, c_im):
+        rows = c_re[0].shape[0]
+        re = jnp.zeros((rows, 256), f32)
+        im = jnp.zeros((rows, 256), f32)
+        for p in range(4):
+            r_re, r_im = (rbuf_0[p, 0], rbuf_0[p, 1]) if f == 0 else (rbuf[p, 2], rbuf[p, 3])
+            re = re + jnp.dot(c_re[p], r_re, preferred_element_type=f32)
+            re = re - jnp.dot(c_im[p], r_im, preferred_element_type=f32)
+            im = im + jnp.dot(c_re[p], r_im, preferred_element_type=f32)
+            im = im + jnp.dot(c_im[p], r_re, preferred_element_type=f32)
+        return re * factor, im * factor
+
+    @pl.loop(20, 24)
+    def _(t):
+        step(t)
+        at = pl.ds(pl.multiple_of((t - 20) * 128, 128), 128)
+        c_re, c_im = [
+            [(cbuf[p, i, at].astype(f32) + delta[p, i, at]).astype(bf16) for p in range(4)] for i in range(2)
+        ]
+        out_v[0, at], out_v[1, at] = product(0, c_re, c_im)
+
+    mult_out = [
+        pltpu.make_async_copy(out_v.at[pl.ds(2 * f, 2)], mult_hbm.at[pl.ds(2 * f, 2)], out_sem.at[1 + f])
+        for f in range(2)
+    ]
+    mult_out[0].start()
+
+    @pl.loop(24, 28)
+    def _(t):
+        step(t)
+        ats = [pl.ds(pl.multiple_of(256 * v + (t - 24) * 64, 64), 64) for v in range(2)]
+        c_re, c_im = [
+            [jnp.concatenate([cbuf[p, i, at] for at in ats], axis=0) for p in range(4)] for i in (2, 3)
+        ]
+        re, im = product(1, c_re, c_im)
+        for v in range(2):
+            out_v[2, ats[v]] = re[64 * v : 64 * (v + 1)]
+            out_v[3, ats[v]] = im[64 * v : 64 * (v + 1)]
+
+    mult_out[1].start()
 
     for p, v, depth, ways in streams:
         for way in STEP:
@@ -324,14 +451,23 @@
             def _():
                 row_wait(p, rbuf.at[p, pl.ds(2, 2)], 1)
 
+    @pl.when(y == 0)
+    def _():
+        for k in range(1, 16):
+            corr_column(k).wait_send()
+
+    @pl.when(core == 0)
+    def _():
+        for k in range(1, 8):
+            corr_row(k).wait_send()
+
     binned_out.wait()
-    for f in range(2):
-        pltpu.make_async_copy(out_v.at[pl.ds(2 * f, 2)], mult_hbm.at[pl.ds(2 * f, 2)], out_sem.at[1 + f]).wait()
+    for one in mult_out:
+        one.wait()
 
 
 def body(data, traces, weight, dest, bins):
     f32, bf16 = jnp.float32, jnp.bfloat16
-    vmem = pl.BlockSpec(memory_space=pltpu.VMEM)
     hbm = pl.BlockSpec(memory_space=pl.ANY)
     dma = pltpu.SemaphoreType.DMA
     return pl.pallas_call(
@@ -340,9 +476,13 @@
             jax.ShapeDtypeStruct((4, 512, 256), bf16),
             jax.ShapeDtypeStruct((4, 512, 256), f32),
         ),
-        in_specs=[vmem, vmem, vmem, vmem, hbm, hbm],
+        in_specs=[pl.BlockSpec(memory_space=pltpu.HBM)] * 6,
         out_specs=(hbm, hbm),
         scratch_shapes=[
+            pltpu.VMEM((8, 128), f32),
+            pltpu.VMEM((1, 512), f32),
+            pltpu.VMEM((1, 512), jnp.int32),
+            pltpu.VMEM((1, 512), jnp.int32),
             pltpu.VMEM((512, 2048), f32),
             pltpu.VMEM((4, 512, 256), bf16),
             pltpu.VMEM((128, 128), f32),
@@ -350,12 +490,17 @@
             pltpu.VMEM((128, 128), f32),
             pltpu.VMEM((128, 128), f32),
             pltpu.VMEM((512, 1024), bf16),
-            pltpu.VMEM((8, 1024, 256), bf16),
+            pltpu.VMEM((4, 1024, 256), bf16),
             pltpu.VMEM((4, 4, 512, 256), bf16),
             pltpu.VMEM((4, 4, 256, 256), bf16),
+            pltpu.VMEM((4, 2, 256, 256), bf16),
+            pltpu.VMEM((4, 128, 128), bf16),
+            pltpu.VMEM((4, 128, 128), bf16),
+            pltpu.VMEM((128, 128), bf16),
+            pltpu.VMEM((4, 2, 512, 256), f32),
             pltpu.VMEM((4, 512, 256), bf16),
             pltpu.VMEM((4, 512, 256), f32),
-            dma((5,)),
+            dma((9,)),
             dma((15,)),
             dma((15,)),
             dma((7,)),
@@ -363,11 +508,15 @@
             dma((8, 4)),
             dma((8, CHUNKS)),
             dma((4, 3)),
-            dma((4, 4)),
+            dma((4, 8)),
+            dma((15,)),
+            dma((4,)),
+            dma((7,)),
+            dma((4,)),
             dma((3,)),
         ],
         compiler_params=pltpu.CompilerParams(
-            collective_id=0, has_side_effects=True, vmem_limit_bytes=40 * 2**20
+            collective_id=0, has_side_effects=True, vmem_limit_bytes=60 * 2**20
         ),
         cost_estimate=pl.CostEstimate(flops=5 * 10**9, bytes_accessed=9 * 2**20, transcendentals=0),
     )(

time: 79 us -> 61.2 us (0.77)
  Pallas kernels: 69.6 us -> 56.4 us
  local copies, waits for them, and re-layouts: 8.43 us -> 3.73 us
    pallas_call x1, Pallas kernels: 69.6 us -> 56.4 us  [body(): pl.pallas_call(kernel, out_shape=(jax.ShapeDtypeStruct((4, 512, 256), bf1...]
    unnamed x14 -> x4, local copies, waits for them, and re-layouts: 8.43 us -> 3.73 us
where the time goes in v2:
time: 61.2 us; the launch traced here: 60.8 us
  Pallas kernels  56.4 us (92%)
  local copies, waits for them, and re-layouts  3.73 us (6%)
  between operations  0.65 us (1%)
    pallas_call x1, Pallas kernels, body(): pl.pallas_call(kernel, out_shape=(jax.ShapeDtypeStruct((4, 512, 256), bf1...  56.4 us
    unnamed x4, local copies, waits for them, and re-layouts  3.73 us

profile of v2, /device:TPU:8, one launch (start us, length us, event | category | flops | bytes accessed | tf_op | source)
XLA Modules:
  0.0 60.8 jit_solution(11872777574991801137)
XLA Ops:
  0.6 56.4 %shard_map.77 = (bf16[4,512,256]{2,1,0:T(8,128)(2,1)}, f32[4,512,256]{2,1,0:T(8,128)}) custom-call(f32[8,128]{1,0:T(8,128)} %constant.2.clone.table_hbm, f32[1,512]{1,0:T(1,128)} %bitcast.3, s32[1,512]{1,0:T(1,128)} %bitcast.4, s32[1,512]{1,0:T(1,128)} %bitcast.5, bf16[4,512,256]{2,1,0:T(8,128)(2,1)} %data_hbm.1, f32[512,2048]{1,0:T(8,128)} %traces_hbm.1), custom_call_target="tpu_custom_call" | custom-call | flops 5000000000 | bytes 9437184 | tf_op jit(solution)/shard_map/pallas_call | solution.py:473
  57.1 0.0 copy-start
  57.1 2.4 %copy.10 = bf16[4,512,256]{2,1,0:T(8,128)(2,1)} copy(bf16[4,512,256]{2,1,0:T(8,128)(2,1)} %get-tuple-element.4) | data formatting | bytes 2097152
  59.5 0.0 copy-done
  59.5 1.3 %copy.11 = f32[4,512,256]{2,1,0:T(8,128)} copy(f32[4,512,256]{2,1,0:T(8,128)S(1)} %copy-done) | data formatting | bytes 4194304
Async XLA Ops:
  57.1 2.4 %copy-start = (f32[4,512,256]{2,1,0:T(8,128)S(1)}, f32[4,512,256]{2,1,0:T(8,128)}, u32[]{:S(2)}) copy-start(f32[4,512,256]{2,1,0:T(8,128)} %get-tuple-element.5) | copy-start | bytes 6291460

commit v3 on v2

v3 whole, which is shorter than its diff:
```python
import functools
import math

import jax
import jax.numpy as jnp
import numpy as np
from jax import lax
from jax.experimental import pallas as pl
from jax.experimental.pallas import tpu as pltpu
from jax.sharding import PartitionSpec as P

MESH = pl.DeviceIdType.MESH
SLOTS = 8
PERIOD = 128
CHUNKS = 16
ROWS_LATE = 9
STRETCH = 3

TREE = {
    (0, 0): ("b", "+y", "-y"),
    (3, 0): ("b",),
    (0, 1): ("f", "+y"),
    (1, 1): ("f", "-y"),
    (0, 3): ("b",),
    (3, 3): ("b",),
    (2, 3): ("-y",),
    (0, 2): ("f", "b"),
    (1, 2): ("+y",),
    (3, 2): ("-y",),
}
STEP = {"f": (1, 0), "b": (3, 0), "+y": (0, 1), "-y": (0, 3)}


def tree_depths():
    depths, front = {(0, 0): 0}, [(0, 0)]
    while front:
        at = front.pop(0)
        for way in TREE.get(at, ()):
            to = ((at[0] + STEP[way][0]) % 4, (at[1] + STEP[way][1]) % 4)
            assert to not in depths
            depths[to] = depths[at] + 1
            front.append(to)
    assert len(depths) == 16
    return depths


DEPTHS = tree_depths()


def table_t():
    n = np.arange(PERIOD)
    rows = []
    for freq in (128, 256):
        angle = (freq * n % 2048) * (2.0 * math.pi / 2048)
        rows += [np.cos(angle), -np.sin(angle)]
    rows = np.stack(rows) * 2048**-0.5
    return np.concatenate([rows, np.zeros((4, PERIOD))]).astype(np.float32)


def kernel(
    table_hbm, weight_hbm, dest_hbm, bins_hbm, data_hbm, traces_hbm, binned_v, out_v,
    table, weight, dest, bins, traces_v, data_v, send_a, recv_a, send_b, recv_b, rows_1h, cols_1h,
    cbuf, rbuf, rbuf_0, corr_c, corr_r, corr_own, delta,
    in_sem, a_send, a_recv, b_send, b_recv, c_send, c_recv, r_send, r_recv,
    cc_send, cc_recv, cr_send, cr_recv,
):
    r = lax.axis_index("rcv")
    s = lax.axis_index("shot")
    x, y = s // 4, s % 4
    z, core = r // 2, r % 2
    f32, bf16 = jnp.float32, jnp.bfloat16

    small_in = [
        pltpu.make_async_copy(one, to, in_sem.at[5 + i])
        for i, (one, to) in enumerate(((dest_hbm, dest), (table_hbm, table), (weight_hbm, weight), (bins_hbm, bins)))
    ]
    trace_in = [
        pltpu.make_async_copy(traces_hbm.at[pl.ds(128 * i, 128)], traces_v.at[pl.ds(128 * i, 128)], in_sem.at[i])
        for i in range(4)
    ]
    data_in = pltpu.make_async_copy(data_hbm, data_v, in_sem.at[4])
    for one in small_in:
        one.start()
    for one in trace_in:
        one.start()
    data_in.start()

    barrier = pltpu.get_barrier_semaphore()
    for k in range(1, 16):
        pl.semaphore_signal(barrier, inc=1, device_id=(r, lax.rem(s + k, 16)), device_id_type=MESH)
    for k in range(1, 8):
        pl.semaphore_signal(barrier, inc=1, device_id=(lax.rem(r + k, 8), s), device_id_type=MESH)

    for one in small_in:
        one.wait()
    owner = dest[...]
    owner = (owner & 15) * 8 + (owner >> 4)
    owner_1h = jnp.where(lax.broadcasted_iota(jnp.int32, (128, 512), 0) == owner, 1.0, 0.0)
    before = jnp.where(
        lax.broadcasted_iota(jnp.int32, (512, 512), 0) < lax.broadcasted_iota(jnp.int32, (512, 512), 1), 1.0, 0.0
    ).astype(bf16)
    owner_1h_b = owner_1h.astype(bf16)
    earlier = jnp.dot(owner_1h_b, before, preferred_element_type=f32)
    slot = jnp.sum(owner_1h * earlier, axis=0, keepdims=True)
    in_slot = lax.broadcasted_iota(jnp.int32, (SLOTS, 512), 0).astype(f32) == slot

    spectra = []
    for i in range(4):
        trace_in[i].wait()
        folded = traces_v[pl.ds(128 * i, 128), 0:PERIOD]
        for b in range(1, 16):
            folded = folded + traces_v[pl.ds(128 * i, 128), PERIOD * b : PERIOD * (b + 1)]
        spectra.append(
            lax.dot_general(
                table[...], folded, (((1,), (1,)), ((), ())),
                precision=lax.Precision.HIGHEST, preferred_element_type=f32,
            )
        )
    spectra = jnp.concatenate(spectra, axis=1)[0:4] * weight[...]
    high = spectra.astype(bf16).astype(f32)
    low = (spectra - high).astype(bf16).astype(f32)
    place = bins[...]
    words = [high[0:1], high[1:2], low[0:1], low[1:2]]
    words += [(place >> 16).astype(f32), ((place >> 8) & 255).astype(f32), (place & 255).astype(f32)]
    words += [jnp.zeros_like(weight[...]), high[2:3], high[3:4], low[2:3], low[3:4]]
    listing = [jnp.where(in_slot, word, 0.0) for word in words]
    listing.append(jnp.zeros((128 - SLOTS * len(words), 512), f32))
    listing = jnp.concatenate(listing, axis=0).astype(bf16)
    send_a[...] = lax.dot_general(owner_1h_b, listing, (((1,), (1,)), ((), ())), preferred_element_type=f32)

    data_in.wait()

    @pl.when(y == 0)
    def _():
        cbuf[x, 0:2] = data_v[0:2]

    @pl.when(core == 0)
    def _():
        rbuf[z, 0:2] = data_v[0:2, 0:256]

    streams = [(dx, v, lax.rem(x + (4 - dx if v == 0 else dx), 4)) for dx in range(4) for v in range(2)]
    up, down = lax.rem(x + 1, 4), lax.rem(x + 3, 4)

    def target(way, v):
        if way == "+y":
            return (r, x * 4 + lax.rem(y + 1, 4))
        if way == "-y":
            return (r, x * 4 + lax.rem(y + 3, 4))
        return (r, (up if (way == "f") == (v == 0) else down) * 4 + y)

    way_index = {way: i for i, way in enumerate(STEP)}

    def column_copy(dx, v, p, j, way):
        comp = (j // 8) * 2 + lax.rem(j, 2)
        start = v * 256 + lax.rem(j // 2, 4) * 64
        ref = cbuf.at[p, comp, pl.ds(pl.multiple_of(start, 64), 64)]
        return pltpu.make_async_remote_copy(
            src_ref=ref, dst_ref=ref, send_sem=c_send.at[2 * dx + v, way_index[way]],
            recv_sem=c_recv.at[2 * p + v, j], device_id=target(way, v), device_id_type=MESH,
        )

    z_up = (lax.rem(z + 1, 4) * 2 + core, s)
    z_down = (lax.rem(z + 3, 4) * 2 + core, s)
    z_core = (z * 2 + 1 - core, s)

    def row_copy(p, k, way):
        ref = rbuf.at[p, k // 2, pl.ds(pl.multiple_of(lax.rem(k, 2) * 128, 128), 128)]
        return pltpu.make_async_remote_copy(
            src_ref=ref, dst_ref=ref, send_sem=r_send.at[p, way], recv_sem=r_recv.at[p, k],
            device_id=(z_up, z_down, z_core)[way], device_id_type=MESH,
        )

    row_panels = [lax.rem(z + 4 - dz, 4) for dz in range(4)]

    def within(t, low, high, first, last, act):
        if low <= first and last <= high:
            act()
        elif first < high and low < last:
            pl.when((t >= low) & (t < high))(act)

    def step(t, first, last):
        for row in range(4):
            @pl.when(y == row)
            def _():
                for dx, v, p in streams:
                    delay = DEPTHS[dx, row] * STRETCH

                    def pass_on():
                        if delay:
                            column_copy(dx, v, p, t - delay, "f").wait_recv()
                        for way in TREE.get((dx, row), ()):
                            column_copy(dx, v, p, t - delay, way).start()

                    within(t, delay, delay + CHUNKS, first, last, pass_on)

        for side in range(2):
            @pl.when(core == side)
            def _():
                for dz, p in enumerate(row_panels):
                    delay = (min(dz, 4 - dz) + side) * STRETCH
                    for begin, k_first in ((0, 0), (ROWS_LATE, 4)):
                        def pass_on():
                            k = t - delay - begin + k_first
                            if delay:
                                row_copy(p, k, 0).wait_recv()
                            if side == 0:
                                row_copy(p, k, 2).start()
                                if dz == 0:
                                    row_copy(p, k, 0).start()
                                    row_copy(p, k, 1).start()
                                elif dz == 1:
                                    pl.when(lax.rem(k, 2) == 0)(lambda: row_copy(p, k, 0).start())
                                elif dz == 3:
                                    pl.when(lax.rem(k, 2) == 1)(lambda: row_copy(p, k, 1).start())

                        within(t, delay + begin, delay + begin + 4, first, last, pass_on)

    def steps(first, last, work=None):
        if last == first + 1:
            step(first, first, last)
            return

        @pl.loop(first, last)
        def _(t):
            step(t, first, last)
            if work:
                work(t)

    def copy_a(k):
        to = lax.rem(s + k, 16)
        return pltpu.make_async_remote_copy(
            src_ref=send_a.at[pl.ds(to * 8, 8)], dst_ref=recv_a.at[pl.ds(s * 8, 8)],
            send_sem=a_send.at[k - 1], recv_sem=a_recv.at[k - 1],
            device_id=(r, to), device_id_type=MESH,
        )

    def copy_b(k):
        to = lax.rem(r + k, 8)
        return pltpu.make_async_remote_copy(
            src_ref=send_b.at[pl.ds(to * 16, 16)], dst_ref=recv_b.at[pl.ds(r * 16, 16)],
            send_sem=b_send.at[k - 1], recv_sem=b_recv.at[k - 1],
            device_id=(to, s), device_id_type=MESH,
        )

    def corr_column(k, along_x):
        to = lax.rem(x + k, 4) * 4 + y if along_x else x * 4 + lax.rem(y + k, 4)
        return pltpu.make_async_remote_copy(
            src_ref=corr_c.at[x], dst_ref=corr_c.at[x], send_sem=cc_send.at[k - 1 + 3 * along_x],
            recv_sem=cc_recv.at[x], device_id=(r, to), device_id_type=MESH,
        )

    def corr_arrived(p):
        pltpu.make_async_remote_copy(
            src_ref=corr_own, dst_ref=corr_c.at[p], send_sem=cc_send.at[0], recv_sem=cc_recv.at[p],
            device_id=(r, lax.rem(s + 1, 16)), device_id_type=MESH,
        ).wait_recv()

    def unpack(packed):
        return jnp.concatenate([packed[:, 0:64], packed[:, 64:128]], axis=0)

    def corr_row(k):
        return pltpu.make_async_remote_copy(
            src_ref=corr_own, dst_ref=corr_r.at[z], send_sem=cr_send.at[k - 1], recv_sem=cr_recv.at[z],
            device_id=(lax.rem(r + k, 8), s), device_id_type=MESH,
        )

    def build_rows(got_t, count):
        for slot_at in range(SLOTS):
            high_row = got_t[32 + slot_at : 33 + slot_at]
            low_row = got_t[40 + slot_at : 41 + slot_at]
            for h in range(count // 256):
                row = jnp.where(high_row == float(h), low_row, -1.0).astype(bf16)
                rows_1h[256 * h : 256 * (h + 1), 128 * slot_at : 128 * (slot_at + 1)] = jnp.where(
                    iota_row == row, jnp.bfloat16(1), jnp.bfloat16(0)
                )

    def build_cols(got, f):
        for slot_at in range(SLOTS):
            column = got[:, 48 + slot_at : 49 + slot_at]
            at_column = iota_col == column
            for i, w in enumerate(range(8 * f, 8 * f + 4)):
                value = got[:, 8 * w + slot_at : 8 * w + slot_at + 1]
                cols_1h[i, 128 * slot_at : 128 * (slot_at + 1)] = jnp.where(at_column, value, jnp.bfloat16(0))

    def added(i, at):
        total = jnp.dot(rows_1h[at], cols_1h[i], preferred_element_type=f32)
        return total + jnp.dot(rows_1h[at], cols_1h[i + 2], preferred_element_type=f32)

    iota_row = lax.broadcasted_iota(jnp.int32, (256, 128), 0).astype(f32).astype(bf16)
    iota_col = lax.broadcasted_iota(jnp.int32, (128, 256), 1).astype(f32).astype(bf16)

    pl.semaphore_wait(barrier, 22)

    for k in range(1, 16):
        copy_a(k).start()
    own = pl.ds(pl.multiple_of(s * 8, 8), 8)
    recv_a[own] = send_a[own]
    steps(0, 4)
    for k in range(1, 16):
        copy_a(k).wait()
    for k in range(8):
        send_b[16 * k : 16 * (k + 1)] = recv_a[pl.ds(k, 16, stride=8)]
    for k in range(1, 8):
        copy_b(k).start()
    own = pl.ds(pl.multiple_of(r * 16, 16), 16)
    recv_b[own] = send_b[own]
    steps(4, 7)
    for k in range(1, 8):
        copy_b(k).wait()
    corr_own[...] = jnp.concatenate([recv_b[0:64, 0:64], recv_b[64:128, 0:64]], axis=1).astype(bf16)

    @pl.when(y == 0)
    def _():
        corr_c[x] = corr_own[...]
        for k in range(1, 4):
            corr_column(k, 0).start()
        for k in range(1, 4):
            corr_column(k, 1).start()

    @pl.when(core == 0)
    def _():
        for k in range(1, 8):
            corr_row(k).start()
        corr_r[z] = corr_own[...]

    steps(7, 8)

    def bin_rows(f, i, at):
        binned_v[2 * f + i, at] = (data_v[2 * f + i, at].astype(f32) + added(i, at)).astype(bf16)

    build_rows(jnp.transpose(recv_b[...]), 512)
    build_cols(recv_b[...].astype(bf16), 1)
    for first, last in ((0, 64), (64, 256)):
        for i in range(2):
            for v in range(2):
                bin_rows(1, i, slice(256 * v + first, 256 * v + last))

        @pl.when(y == 0)
        def _():
            for v in range(2):
                at = slice(256 * v + first, 256 * v + last)
                cbuf[x, 2:4, at] = binned_v[2:4, at]

        @pl.when(core == 0)
        def _():
            rbuf[z, 2:4, first:last] = binned_v[2:4, first:last]

        if first == 0:
            steps(8, 9)
    steps(9, 10)
    build_cols(recv_b[...].astype(bf16), 0)
    bin_rows(0, 0, slice(0, 512))
    steps(10, 11)

    @pl.when(y != 0)
    def _():
        corr_arrived(x)
        for k in range(1, 4):
            corr_column(k, 1).start()

    bin_rows(0, 1, slice(0, 512))
    steps(11, 12)

    for p in range(4):
        @pl.when((core != 0) | (z != p))
        def _():
            pltpu.make_async_remote_copy(
                src_ref=corr_own, dst_ref=corr_r.at[p], send_sem=cr_send.at[0], recv_sem=cr_recv.at[p],
                device_id=(lax.rem(r + 1, 8), s), device_id_type=MESH,
            ).wait_recv()

    def correct_rows(t):
        p = t - 12
        got = unpack(corr_r[p])
        build_rows(jnp.transpose(got.astype(f32)), 256)
        build_cols(got, 0)
        for i in range(2):
            rbuf_0[p, i] = (rbuf[p, i].astype(f32) + added(i, slice(0, 256))).astype(bf16)

    def correct_columns(t):
        p, i = (t - 16) // 2, lax.rem(t, 2)

        @pl.when(i == 0)
        def _():
            @pl.when(x != p)
            def _():
                corr_arrived(p)

            got = unpack(corr_c[p])
            build_rows(jnp.transpose(got.astype(f32)), 512)
            build_cols(got, 0)

        delta[p, i] = added(i, slice(0, 512))

    steps(12, 16, correct_rows)
    steps(16, 24, correct_columns)

    factor = 2048**-0.5

    def product(f, c_re, c_im):
        rows = c_re[0].shape[0]
        re = jnp.zeros((rows, 256), f32)
        im = jnp.zeros((rows, 256), f32)
        for p in range(4):
            r_re, r_im = (rbuf_0[p, 0], rbuf_0[p, 1]) if f == 0 else (rbuf[p, 2], rbuf[p, 3])
            re = re + jnp.dot(c_re[p], r_re, preferred_element_type=f32)
            re = re - jnp.dot(c_im[p], r_im, preferred_element_type=f32)
            im = im + jnp.dot(c_re[p], r_im, preferred_element_type=f32)
            im = im + jnp.dot(c_im[p], r_re, preferred_element_type=f32)
        return re * factor, im * factor

    def multiply(t):
        at = pl.ds(pl.multiple_of((t - 24) * 128, 128), 128)
        c_re, c_im = [
            [(cbuf[p, i, at].astype(f32) + delta[p, i, at]).astype(bf16) for p in range(4)] for i in range(2)
        ]
        out_v[0, at], out_v[1, at] = product(0, c_re, c_im)
        ats = [pl.ds(pl.multiple_of(256 * v + (t - 24) * 64, 64), 64) for v in range(2)]
        c_re, c_im = [
            [jnp.concatenate([cbuf[p, i, at] for at in ats], axis=0) for p in range(4)] for i in (2, 3)
        ]
        re, im = product(1, c_re, c_im)
        for v in range(2):
            out_v[2, ats[v]] = re[64 * v : 64 * (v + 1)]
            out_v[3, ats[v]] = im[64 * v : 64 * (v + 1)]

    steps(24, 28, multiply)

    for row in range(4):
        @pl.when(y == row)
        def _():
            for dx, v, p in streams:
                half = cbuf.at[p, :, pl.ds(v * 256, 256)]
                for way in TREE.get((dx, row), ()):
                    pltpu.make_async_remote_copy(
                        src_ref=half, dst_ref=half, send_sem=c_send.at[2 * dx + v, way_index[way]],
                        recv_sem=c_recv.at[2 * p + v, 0], device_id=target(way, v), device_id_type=MESH,
                    ).wait_send()

    def row_wait(p, ref, way):
        pltpu.make_async_remote_copy(
            src_ref=ref, dst_ref=ref, send_sem=r_send.at[p, way], recv_sem=r_recv.at[p, 0],
            device_id=(z_up, z_down, z_core)[way], device_id_type=MESH,
        ).wait_send()

    @pl.when(core == 0)
    def _():
        for dz, p in enumerate(row_panels):
            row_wait(p, rbuf.at[p], 2)
            if dz == 0:
                row_wait(p, rbuf.at[p], 0)
                row_wait(p, rbuf.at[p], 1)
            elif dz == 1:
                row_wait(p, rbuf.at[p, pl.ds(0, 2)], 0)
            elif dz == 3:
                row_wait(p, rbuf.at[p, pl.ds(2, 2)], 1)

    @pl.when(y == 0)
    def _():
        for k in range(1, 4):
            corr_column(k, 0).wait_send()

    for k in range(1, 4):
        corr_column(k, 1).wait_send()

    @pl.when(core == 0)
    def _():
        for k in range(1, 8):
            corr_row(k).wait_send()


def body(data, traces, weight, dest, bins):
    f32, bf16 = jnp.float32, jnp.bfloat16
    dma = pltpu.SemaphoreType.DMA
    return pl.pallas_call(
        kernel,
        out_shape=(
            pltpu.VMEM((4, 512, 256), bf16),
            pltpu.VMEM((4, 512, 256), f32),
        ),
        in_specs=[pl.BlockSpec(memory_space=pltpu.HBM)] * 6,
        out_specs=(pl.BlockSpec(memory_space=pltpu.VMEM),) * 2,
        scratch_shapes=[
            pltpu.VMEM((8, 128), f32),
            pltpu.VMEM((1, 512), f32),
            pltpu.VMEM((1, 512), jnp.int32),
            pltpu.VMEM((1, 512), jnp.int32),
            pltpu.VMEM((512, 2048), f32),
            pltpu.VMEM((4, 512, 256), bf16),
            pltpu.VMEM((128, 128), f32),
            pltpu.VMEM((128, 128), f32),
            pltpu.VMEM((128, 128), f32),
            pltpu.VMEM((128, 128), f32),
            pltpu.VMEM((512, 1024), bf16),
            pltpu.VMEM((4, 1024, 256), bf16),
            pltpu.VMEM((4, 4, 512, 256), bf16),
            pltpu.VMEM((4, 4, 256, 256), bf16),
            pltpu.VMEM((4, 2, 256, 256), bf16),
            pltpu.VMEM((4, 64, 128), bf16),
            pltpu.VMEM((4, 64, 128), bf16),
            pltpu.VMEM((64, 128), bf16),
            pltpu.VMEM((4, 2, 512, 256), f32),
            dma((9,)),
            dma((15,)),
            dma((15,)),
            dma((7,)),
            dma((7,)),
            dma((8, 4)),
            dma((8, CHUNKS)),
            dma((4, 3)),
            dma((4, 8)),
            dma((6,)),
            dma((4,)),
            dma((7,)),
            dma((4,)),
        ],
        compiler_params=pltpu.CompilerParams(
            collective_id=0, has_side_effects=True, vmem_limit_bytes=40 * 2**20
        ),
        cost_estimate=pl.CostEstimate(flops=5 * 10**9, bytes_accessed=9 * 2**20, transcendentals=0),
    )(
        *(
            pltpu.with_memory_space_constraint(one, pltpu.HBM)
            for one in (
                jnp.asarray(table_t()),
                weight.reshape(1, 512),
                dest.reshape(1, 512),
                bins.reshape(1, 512),
                data,
                traces,
            )
        )
    )


def solution(mesh):
    placed = (
        P(None, "rcv", "shot"),
        P(("rcv", "shot"), None),
        P(("rcv", "shot")),
        P(("rcv", "shot"), None),
        P(("rcv", "shot")),
    )
    return jax.shard_map(
        body,
        mesh=mesh,
        in_specs=placed,
        out_specs=(P(None, "rcv", "shot"), P(None, "rcv", "shot")),
        check_vma=False,
    )
```

time: 61.2 us -> 51.9 us (0.85)
  Pallas kernels: 56.4 us -> 48.9 us
  local copies, waits for them, and re-layouts: 3.73 us -> 2.29 us
    pallas_call x1, Pallas kernels: 56.4 us -> 48.9 us  [body(): pl.pallas_call(kernel, out_shape=(pltpu.VMEM((4, 512, 256), bf16), pltpu....]
    unnamed x4 -> x2, local copies, waits for them, and re-layouts: 3.73 us -> 2.29 us
where the time goes in v3:
time: 51.9 us; the launch traced here: 51.8 us
  Pallas kernels  48.9 us (94%)
  local copies, waits for them, and re-layouts  2.29 us (4%)
  between operations  0.64 us (1%)
    pallas_call x1, Pallas kernels, body(): pl.pallas_call(kernel, out_shape=(pltpu.VMEM((4, 512, 256), bf16), pltpu....  48.9 us
    unnamed x2, local copies, waits for them, and re-layouts  2.29 us

profile of v3, /device:TPU:8, one launch (start us, length us, event | category | flops | bytes accessed | tf_op | source)
XLA Modules:
  0.0 51.8 jit_solution(7853745839120803201)
XLA Ops:
  0.6 48.9 %shard_map.77 = (bf16[4,512,256]{2,1,0:T(8,128)(2,1)S(1)}, f32[4,512,256]{2,1,0:T(8,128)S(1)}) custom-call(f32[8,128]{1,0:T(8,128)} %constant.2.clone.table_hbm, f32[1,512]{1,0:T(1,128)} %bitcast.3, s32[1,512]{1,0:T(1,128)} %bitcast.4, s32[1,512]{1,0:T(1,128)} %bitcast.5, bf16[4,512,256]{2,1,0:T(8,128)(2,1)} %data_hbm.1, f32[512,2048]{1,0:T(8,128)} %traces_hbm.1), custom_call_target="tpu_custom_call" | custom-call | flops 5000000000 | bytes 9437184 | tf_op jit(solution)/shard_map/pallas_call | solution.py:475
  49.5 1.0 %copy.10 = bf16[4,512,256]{2,1,0:T(8,128)(2,1)} copy(bf16[4,512,256]{2,1,0:T(8,128)(2,1)S(1)} %get-tuple-element.2) | data formatting | bytes 2097152
  50.5 1.3 %copy.11 = f32[4,512,256]{2,1,0:T(8,128)} copy(f32[4,512,256]{2,1,0:T(8,128)S(1)} %get-tuple-element.3) | data formatting | bytes 4194304

commit v4 on v3

--- a/solution.py
+++ b/solution.py
@@ -10,6 +10,8 @@
 from jax.sharding import PartitionSpec as P
 
 MESH = pl.DeviceIdType.MESH
+FAR_SHOT = (10, 9, 11, 6, 7, 5, 14, 13, 15, 8, 2, 3, 1, 4, 12)
+FAR_RCV = (4, 5, 3, 2, 6, 7, 1)
 SLOTS = 8
 PERIOD = 128
 CHUNKS = 16
@@ -69,6 +71,12 @@
     x, y = s // 4, s % 4
     z, core = r // 2, r % 2
     f32, bf16 = jnp.float32, jnp.bfloat16
+
+    barrier = pltpu.get_barrier_semaphore()
+    for k in FAR_SHOT:
+        pl.semaphore_signal(barrier, inc=1, device_id=(r, lax.rem(s + k, 16)), device_id_type=MESH)
+    for k in FAR_RCV:
+        pl.semaphore_signal(barrier, inc=1, device_id=(lax.rem(r + k, 8), s), device_id_type=MESH)
 
     small_in = [
         pltpu.make_async_copy(one, to, in_sem.at[5 + i])
@@ -85,12 +93,6 @@
         one.start()
     data_in.start()
 
-    barrier = pltpu.get_barrier_semaphore()
-    for k in range(1, 16):
-        pl.semaphore_signal(barrier, inc=1, device_id=(r, lax.rem(s + k, 16)), device_id_type=MESH)
-    for k in range(1, 8):
-        pl.semaphore_signal(barrier, inc=1, device_id=(lax.rem(r + k, 8), s), device_id_type=MESH)
-
     for one in small_in:
         one.wait()
     owner = dest[...]
@@ -198,9 +200,11 @@
             def _():
                 for dz, p in enumerate(row_panels):
                     delay = (min(dz, 4 - dz) + side) * STRETCH
-                    for begin, k_first in ((0, 0), (ROWS_LATE, 4)):
+                    for begin, k_first in ((0, 0), (0, 1), (0, 2), (0, 3), (ROWS_LATE, 4)):
                         def pass_on():
                             k = t - delay - begin + k_first
+                            if begin == 0:
+                                k = jnp.int32(k_first)
                             if delay:
                                 row_copy(p, k, 0).wait_recv()
                             if side == 0:
@@ -213,11 +217,17 @@
                                 elif dz == 3:
                                     pl.when(lax.rem(k, 2) == 1)(lambda: row_copy(p, k, 1).start())
 
-                        within(t, delay + begin, delay + begin + 4, first, last, pass_on)
+                        if begin:
+                            within(t, delay + begin, delay + begin + 4, first, last, pass_on)
+                        else:
+                            at = delay + k_first // 2
+                            within(t, at, at + 1, first, last, pass_on)
 
     def steps(first, last, work=None):
         if last == first + 1:
             step(first, first, last)
+            if work:
+                work(first)
             return
 
         @pl.loop(first, last)
@@ -291,20 +301,20 @@
 
     pl.semaphore_wait(barrier, 22)
 
-    for k in range(1, 16):
+    for k in FAR_SHOT:
         copy_a(k).start()
     own = pl.ds(pl.multiple_of(s * 8, 8), 8)
     recv_a[own] = send_a[own]
-    steps(0, 4)
+    steps(0, 3)
     for k in range(1, 16):
         copy_a(k).wait()
     for k in range(8):
         send_b[16 * k : 16 * (k + 1)] = recv_a[pl.ds(k, 16, stride=8)]
-    for k in range(1, 8):
+    for k in FAR_RCV:
         copy_b(k).start()
     own = pl.ds(pl.multiple_of(r * 16, 16), 16)
     recv_b[own] = send_b[own]
-    steps(4, 7)
+    steps(3, 6)
     for k in range(1, 8):
         copy_b(k).wait()
     corr_own[...] = jnp.concatenate([recv_b[0:64, 0:64], recv_b[64:128, 0:64]], axis=1).astype(bf16)
@@ -323,7 +333,7 @@
             corr_row(k).start()
         corr_r[z] = corr_own[...]
 
-    steps(7, 8)
+    steps(6, 7)
 
     def bin_rows(f, i, at):
         binned_v[2 * f + i, at] = (data_v[2 * f + i, at].astype(f32) + added(i, at)).astype(bf16)
@@ -346,20 +356,11 @@
             rbuf[z, 2:4, first:last] = binned_v[2:4, first:last]
 
         if first == 0:
-            steps(8, 9)
+            steps(7, 9)
     steps(9, 10)
     build_cols(recv_b[...].astype(bf16), 0)
-    bin_rows(0, 0, slice(0, 512))
-    steps(10, 11)
-
-    @pl.when(y != 0)
-    def _():
-        corr_arrived(x)
-        for k in range(1, 4):
-            corr_column(k, 1).start()
-
-    bin_rows(0, 1, slice(0, 512))
-    steps(11, 12)
+    for i in range(2):
+        bin_rows(0, i, slice(0, 512))
 
     for p in range(4):
         @pl.when((core != 0) | (z != p))
@@ -370,7 +371,7 @@
             ).wait_recv()
 
     def correct_rows(t):
-        p = t - 12
+        p = t - 10
         got = unpack(corr_r[p])
         build_rows(jnp.transpose(got.astype(f32)), 256)
         build_cols(got, 0)
@@ -378,7 +379,7 @@
             rbuf_0[p, i] = (rbuf[p, i].astype(f32) + added(i, slice(0, 256))).astype(bf16)
 
     def correct_columns(t):
-        p, i = (t - 16) // 2, lax.rem(t, 2)
+        p, i = (t - 14) // 2, lax.rem(t, 2)
 
         @pl.when(i == 0)
         def _():
@@ -392,8 +393,16 @@
 
         delta[p, i] = added(i, slice(0, 512))
 
-    steps(12, 16, correct_rows)
-    steps(16, 24, correct_columns)
+    steps(10, 11, correct_rows)
+
+    @pl.when(y != 0)
+    def _():
+        corr_arrived(x)
+        for k in range(1, 4):
+            corr_column(k, 1).start()
+
+    steps(11, 14, correct_rows)
+    steps(14, 22, correct_columns)
 
     factor = 2048**-0.5
 
@@ -409,12 +418,14 @@
             im = im + jnp.dot(c_im[p], r_re, preferred_element_type=f32)
         return re * factor, im * factor
 
-    def multiply(t):
-        at = pl.ds(pl.multiple_of((t - 24) * 128, 128), 128)
+    def multiply_0(t):
+        at = pl.ds(pl.multiple_of((t - 22) * 128, 128), 128)
         c_re, c_im = [
             [(cbuf[p, i, at].astype(f32) + delta[p, i, at]).astype(bf16) for p in range(4)] for i in range(2)
         ]
         out_v[0, at], out_v[1, at] = product(0, c_re, c_im)
+
+    def multiply_1(t):
         ats = [pl.ds(pl.multiple_of(256 * v + (t - 24) * 64, 64), 64) for v in range(2)]
         c_re, c_im = [
             [jnp.concatenate([cbuf[p, i, at] for at in ats], axis=0) for p in range(4)] for i in (2, 3)
@@ -424,7 +435,13 @@
             out_v[2, ats[v]] = re[64 * v : 64 * (v + 1)]
             out_v[3, ats[v]] = im[64 * v : 64 * (v + 1)]
 
-    steps(24, 28, multiply)
+    def multiply_both(t):
+        multiply_0(t)
+        multiply_1(t)
+
+    steps(22, 24, multiply_0)
+    steps(24, 26, multiply_both)
+    steps(26, 28, multiply_1)
 
     for row in range(4):
         @pl.when(y == row)
@@ -469,10 +486,22 @@
             corr_row(k).wait_send()
 
 
+def write_out(binned_v, out_v, binned_hbm, mult_hbm, sem):
+    copies = [
+        pltpu.make_async_copy(one.at[i], to.at[i], sem.at[n, i])
+        for n, (one, to) in enumerate(((out_v, mult_hbm), (binned_v, binned_hbm)))
+        for i in range(4)
+    ]
+    for one in copies:
+        one.start()
+    for one in copies:
+        one.wait()
+
+
 def body(data, traces, weight, dest, bins):
     f32, bf16 = jnp.float32, jnp.bfloat16
     dma = pltpu.SemaphoreType.DMA
-    return pl.pallas_call(
+    results = pl.pallas_call(
         kernel,
         out_shape=(
             pltpu.VMEM((4, 512, 256), bf16),
@@ -531,6 +560,17 @@
             )
         )
     )
+    return pl.pallas_call(
+        write_out,
+        out_shape=(
+            jax.ShapeDtypeStruct((4, 512, 256), bf16),
+            jax.ShapeDtypeStruct((4, 512, 256), f32),
+        ),
+        in_specs=[pl.BlockSpec(memory_space=pltpu.VMEM)] * 2,
+        out_specs=(pl.BlockSpec(memory_space=pltpu.HBM),) * 2,
+        scratch_shapes=[dma((2, 4))],
+        cost_estimate=pl.CostEstimate(flops=0, bytes_accessed=3 * 2**20, transcendentals=0),
+    )(*(pltpu.with_memory_space_constraint(one, pltpu.VMEM) for one in results))
 
 
 def solution(mesh):

time: 51.9 us -> 51.6 us (level)
  local copies, waits for them, and re-layouts: 2.29 us -> 0 us
  Pallas kernels: 48.9 us -> 50.8 us
    unnamed x2 -> x0, local copies, waits for them, and re-layouts: 2.29 us -> none
    pallas_call x0 -> x1, Pallas kernels: none -> 1.72 us  [body(): pl.pallas_call(write_out, out_shape=(jax.ShapeDtypeStruct((4, 512, 256),...]
where the time goes in v4:
time: 51.6 us; the launch traced here: 51.5 us
  Pallas kernels  50.8 us (98%)
  between operations  0.64 us (1%)
    pallas_call x1, Pallas kernels, body(): pl.pallas_call(kernel, out_shape=(pltpu.VMEM((4, 512, 256), bf16), pltpu....  49.1 us
    pallas_call x1, Pallas kernels, body(): pl.pallas_call(write_out, out_shape=(jax.ShapeDtypeStruct((4, 512, 256),...  1.72 us

profile of v4, /device:TPU:8, one launch (start us, length us, event | category | flops | bytes accessed | tf_op | source)
XLA Modules:
  0.0 51.5 jit_solution(16109794102945036215)
XLA Ops:
  0.6 49.1 %shard_map.77 = (bf16[4,512,256]{2,1,0:T(8,128)(2,1)S(1)}, f32[4,512,256]{2,1,0:T(8,128)S(1)}) custom-call(f32[8,128]{1,0:T(8,128)} %constant.2.clone.table_hbm, f32[1,512]{1,0:T(1,128)} %bitcast.3, s32[1,512]{1,0:T(1,128)} %bitcast.4, s32[1,512]{1,0:T(1,128)} %bitcast.5, bf16[4,512,256]{2,1,0:T(8,128)(2,1)} %data_hbm.1, f32[512,2048]{1,0:T(8,128)} %traces_hbm.1), custom_call_target="tpu_custom_call" | custom-call | flops 5000000000 | bytes 9437184 | tf_op jit(solution)/shard_map/pallas_call | solution.py:504
  49.8 1.7 %shard_map.78 = (bf16[4,512,256]{2,1,0:T(8,128)(2,1)}, f32[4,512,256]{2,1,0:T(8,128)}) custom-call(bf16[4,512,256]{2,1,0:T(8,128)(2,1)S(1)} %get-tuple-element.4.binned_v, f32[4,512,256]{2,1,0:T(8,128)S(1)} %get-tuple-element.5.out_v), custom_call_target="tpu_custom_call" | custom-call | bytes 3145728 | tf_op jit(solution)/shard_map/pallas_call | solution.py:563

commit v5 on v4

--- a/solution.py
+++ b/solution.py
@@ -223,19 +223,6 @@
                             at = delay + k_first // 2
                             within(t, at, at + 1, first, last, pass_on)
 
-    def steps(first, last, work=None):
-        if last == first + 1:
-            step(first, first, last)
-            if work:
-                work(first)
-            return
-
-        @pl.loop(first, last)
-        def _(t):
-            step(t, first, last)
-            if work:
-                work(t)
-
     def copy_a(k):
         to = lax.rem(s + k, 16)
         return pltpu.make_async_remote_copy(
@@ -305,42 +292,10 @@
         copy_a(k).start()
     own = pl.ds(pl.multiple_of(s * 8, 8), 8)
     recv_a[own] = send_a[own]
-    steps(0, 3)
-    for k in range(1, 16):
-        copy_a(k).wait()
-    for k in range(8):
-        send_b[16 * k : 16 * (k + 1)] = recv_a[pl.ds(k, 16, stride=8)]
-    for k in FAR_RCV:
-        copy_b(k).start()
-    own = pl.ds(pl.multiple_of(r * 16, 16), 16)
-    recv_b[own] = send_b[own]
-    steps(3, 6)
-    for k in range(1, 8):
-        copy_b(k).wait()
-    corr_own[...] = jnp.concatenate([recv_b[0:64, 0:64], recv_b[64:128, 0:64]], axis=1).astype(bf16)
-
-    @pl.when(y == 0)
-    def _():
-        corr_c[x] = corr_own[...]
-        for k in range(1, 4):
-            corr_column(k, 0).start()
-        for k in range(1, 4):
-            corr_column(k, 1).start()
-
-    @pl.when(core == 0)
-    def _():
-        for k in range(1, 8):
-            corr_row(k).start()
-        corr_r[z] = corr_own[...]
-
-    steps(6, 7)
-
     def bin_rows(f, i, at):
         binned_v[2 * f + i, at] = (data_v[2 * f + i, at].astype(f32) + added(i, at)).astype(bf16)
 
-    build_rows(jnp.transpose(recv_b[...]), 512)
-    build_cols(recv_b[...].astype(bf16), 1)
-    for first, last in ((0, 64), (64, 256)):
+    def bin_second(first, last):
         for i in range(2):
             for v in range(2):
                 bin_rows(1, i, slice(256 * v + first, 256 * v + last))
@@ -355,20 +310,59 @@
         def _():
             rbuf[z, 2:4, first:last] = binned_v[2:4, first:last]
 
-        if first == 0:
-            steps(7, 9)
-    steps(9, 10)
-    build_cols(recv_b[...].astype(bf16), 0)
-    for i in range(2):
-        bin_rows(0, i, slice(0, 512))
-
-    for p in range(4):
-        @pl.when((core != 0) | (z != p))
-        def _():
-            pltpu.make_async_remote_copy(
-                src_ref=corr_own, dst_ref=corr_r.at[p], send_sem=cr_send.at[0], recv_sem=cr_recv.at[p],
-                device_id=(lax.rem(r + 1, 8), s), device_id_type=MESH,
-            ).wait_recv()
+    def exchange_over_rcv():
+        for k in range(1, 16):
+            copy_a(k).wait()
+        for k in range(8):
+            send_b[16 * k : 16 * (k + 1)] = recv_a[pl.ds(k, 16, stride=8)]
+        for k in FAR_RCV:
+            copy_b(k).start()
+        own = pl.ds(pl.multiple_of(r * 16, 16), 16)
+        recv_b[own] = send_b[own]
+
+    def send_corrections():
+        for k in range(1, 8):
+            copy_b(k).wait()
+        corr_own[...] = jnp.concatenate([recv_b[0:64, 0:64], recv_b[64:128, 0:64]], axis=1).astype(bf16)
+
+        @pl.when(y == 0)
+        def _():
+            corr_c[x] = corr_own[...]
+            for k in range(1, 4):
+                corr_column(k, 0).start()
+            for k in range(1, 4):
+                corr_column(k, 1).start()
+
+        @pl.when(core == 0)
+        def _():
+            for k in range(1, 8):
+                corr_row(k).start()
+            corr_r[z] = corr_own[...]
+
+    def bin_first_rows():
+        build_rows(jnp.transpose(recv_b[...]), 512)
+        build_cols(recv_b[...].astype(bf16), 1)
+        bin_second(0, 64)
+
+    def bin_first():
+        build_cols(recv_b[...].astype(bf16), 0)
+        for i in range(2):
+            bin_rows(0, i, slice(0, 512))
+
+        for p in range(4):
+            @pl.when((core != 0) | (z != p))
+            def _():
+                pltpu.make_async_remote_copy(
+                    src_ref=corr_own, dst_ref=corr_r.at[p], send_sem=cr_send.at[0], recv_sem=cr_recv.at[p],
+                    device_id=(lax.rem(r + 1, 8), s), device_id_type=MESH,
+                ).wait_recv()
+
+    def relay_corrections():
+        @pl.when(y != 0)
+        def _():
+            corr_arrived(x)
+            for k in range(1, 4):
+                corr_column(k, 1).start()
 
     def correct_rows(t):
         p = t - 10
@@ -392,17 +386,6 @@
             build_cols(got, 0)
 
         delta[p, i] = added(i, slice(0, 512))
-
-    steps(10, 11, correct_rows)
-
-    @pl.when(y != 0)
-    def _():
-        corr_arrived(x)
-        for k in range(1, 4):
-            corr_column(k, 1).start()
-
-    steps(11, 14, correct_rows)
-    steps(14, 22, correct_columns)
 
     factor = 2048**-0.5
 
@@ -435,13 +418,20 @@
             out_v[2, ats[v]] = re[64 * v : 64 * (v + 1)]
             out_v[3, ats[v]] = im[64 * v : 64 * (v + 1)]
 
-    def multiply_both(t):
-        multiply_0(t)
-        multiply_1(t)
-
-    steps(22, 24, multiply_0)
-    steps(24, 26, multiply_both)
-    steps(26, 28, multiply_1)
+    once = {
+        2: exchange_over_rcv, 5: send_corrections, 6: bin_first_rows, 8: lambda: bin_second(64, 256),
+        9: bin_first, 10: relay_corrections,
+    }
+
+    @pl.loop(0, 28)
+    def _(t):
+        step(t, 0, 28)
+        for turn, work in once.items():
+            pl.when(t == turn)(work)
+        for first, last, work in (
+            (10, 14, correct_rows), (14, 22, correct_columns), (22, 26, multiply_0), (24, 28, multiply_1)
+        ):
+            pl.when((t >= first) & (t < last))(functools.partial(work, t))
 
     for row in range(4):
         @pl.when(y == row)

time: 51.6 us -> 53.7 us (1.041)
  Pallas kernels: 50.8 us -> 52.5 us
    pallas_call x1, Pallas kernels: 49.1 us -> 50.8 us  [body(): pl.pallas_call(kernel, out_shape=(pltpu.VMEM((4, 512, 256), bf16), pltpu....]
where the time goes in v5:
time: 53.7 us; the launch traced here: 53.1 us
  Pallas kernels  52.5 us (98%)
  between operations  0.64 us (1%)
    pallas_call x1, Pallas kernels, body(): pl.pallas_call(kernel, out_shape=(pltpu.VMEM((4, 512, 256), bf16), pltpu....  50.8 us
    pallas_call x1, Pallas kernels, body(): pl.pallas_call(write_out, out_shape=(jax.ShapeDtypeStruct((4, 512, 256),...  1.72 us

profile of v5, /device:TPU:8, one launch (start us, length us, event | category | flops | bytes accessed | tf_op | source)
XLA Modules:
  0.0 53.1 jit_solution(4076294281048107847)
XLA Ops:
  0.6 50.8 %shard_map.77 = (bf16[4,512,256]{2,1,0:T(8,128)(2,1)S(1)}, f32[4,512,256]{2,1,0:T(8,128)S(1)}) custom-call(f32[8,128]{1,0:T(8,128)} %constant.2.clone.table_hbm, f32[1,512]{1,0:T(1,128)} %bitcast.3, s32[1,512]{1,0:T(1,128)} %bitcast.4, s32[1,512]{1,0:T(1,128)} %bitcast.5, bf16[4,512,256]{2,1,0:T(8,128)(2,1)} %data_hbm.1, f32[512,2048]{1,0:T(8,128)} %traces_hbm.1), custom_call_target="tpu_custom_call" | custom-call | flops 5000000000 | bytes 9437184 | tf_op jit(solution)/shard_map/pallas_call | solution.py:494
  51.4 1.7 %shard_map.78 = (bf16[4,512,256]{2,1,0:T(8,128)(2,1)}, f32[4,512,256]{2,1,0:T(8,128)}) custom-call(bf16[4,512,256]{2,1,0:T(8,128)(2,1)S(1)} %get-tuple-element.4.binned_v, f32[4,512,256]{2,1,0:T(8,128)S(1)} %get-tuple-element.5.out_v), custom_call_target="tpu_custom_call" | custom-call | bytes 3145728 | tf_op jit(solution)/shard_map/pallas_call | solution.py:553
